TPU v7x, 256 devices: a whole 4x4x8 slice. The times are simulated.
256 devices in a mesh: dp: 64 (over x, z, core), head: 4 (over y).
Axes of the slice: x: 4, y: 4, z: 8, core: 2. Of those that a mesh axis runs over, the one named last changes fastest.
Arguments:
- queries: bfloat16 [2, 16384, 8192], P(None, 'dp', 'head'), may hold values from -5 to 5
- keys: bfloat16 [2, 16384, 1024], P(None, 'dp', 'head'), may hold values from -5 to 5
- values: bfloat16 [2, 16384, 1024], P(None, 'dp', 'head'), may hold values from -5 to 5
- prefix_keys: bfloat16 [2, 128, 1024], P(None, None, 'head'), may hold values from -5 to 5
- prefix_values: bfloat16 [2, 128, 1024], P(None, None, 'head'), may hold values from -5 to 5
- dout: bfloat16 [2, 16384, 8192], P(None, 'dp', 'head'), may hold values from -6 to 6
- key_weight: bfloat16 [2, 8192, 1024], P(None, 'dp', 'head'), may hold values from -0.125 to 0.125
- value_weight: bfloat16 [2, 8192, 1024], P(None, 'dp', 'head'), may hold values from -0.125 to 0.125
Outputs:
- grad_queries: bfloat16 [2, 16384, 8192], P(None, 'dp', 'head')
- grad_input: bfloat16 [2, 16384, 8192], P(None, 'dp', 'head')
- grad_prefix_keys: float32 [2, 128, 1024], P(None, None, 'head')
- grad_prefix_values: float32 [2, 128, 1024], P(None, None, 'head')
All inputs are finite; a program needn't handle non-finite values.
Results may differ from a plain program's by a relative error of at most 0.013.
Values may be sent and summed in bfloat16 or wider, within the bound.
No kernel may reach another device: no remote copies, remote signals or barrier semaphores. Data moves between devices by JAX's collectives and lax.ppermute only.
A program may use at most 128 MiB of HBM per device.

v0:
```python
import jax
import jax.numpy as jnp
from jax import lax
from jax.sharding import PartitionSpec as P

QH = 64
KVH = 8
HD = 128
LEN = 256


def attend_back(queries, keys, values, pre_keys, pre_values, dout):
    seq_count, length, head_count, group_size, head_width = queries.shape
    prefix = pre_keys.shape[0]
    score_scale = head_width ** (-0.5)
    all_keys = jnp.concatenate([pre_keys[None], keys], axis=1)
    all_values = jnp.concatenate([pre_values[None], values], axis=1)
    position = jnp.arange(length)
    key_position = jnp.arange(prefix + length) - prefix
    visible = key_position[None, :] <= position[:, None]
    scores = (
        jnp.einsum("bskgh,bmkh->bkgsm", queries, all_keys, preferred_element_type=jnp.float32)
        * score_scale
    )
    scores = jnp.where(visible, scores, -1e30)
    row_peak = jnp.max(scores, axis=-1, keepdims=True)
    exp_scores = jnp.exp(scores - row_peak)
    probs = exp_scores / jnp.sum(exp_scores, axis=-1, keepdims=True)
    probs_low = probs.astype(jnp.bfloat16)
    attended = jnp.einsum(
        "bkgsm,bmkh->bskgh", probs_low, all_values, preferred_element_type=jnp.float32
    )
    row_delta = jnp.transpose(jnp.sum(dout.astype(jnp.float32) * attended, axis=-1), (0, 2, 3, 1))
    dprobs = jnp.einsum("bskgh,bmkh->bkgsm", dout, all_values, preferred_element_type=jnp.float32)
    dscores = (probs * (dprobs - row_delta[..., None]) * score_scale).astype(jnp.bfloat16)
    grad_query = jnp.einsum(
        "bkgsm,bmkh->bskgh", dscores, all_keys, preferred_element_type=jnp.float32
    ).astype(jnp.bfloat16)
    key_terms = jnp.einsum(
        "bkgsm,bskgh->bmkh", dscores, queries, preferred_element_type=jnp.float32
    )
    value_terms = jnp.einsum(
        "bkgsm,bskgh->bmkh", probs_low, dout, preferred_element_type=jnp.float32
    )
    return (
        grad_query,
        key_terms[:, prefix:].astype(jnp.bfloat16),
        value_terms[:, prefix:].astype(jnp.bfloat16),
        jnp.sum(key_terms[:, :prefix], axis=0),
        jnp.sum(value_terms[:, :prefix], axis=0),
    )


def project_rows(flat, weight_rows):
    return lax.dot_general(
        flat, weight_rows, (((1,), (1,)), ((), ())), preferred_element_type=jnp.float32
    )


def shards(queries, keys, values, prefix_keys, prefix_values, dout, key_weight, value_weight):
    layer_count = queries.shape[0]
    tokens_here = queries.shape[1]
    seq_count = tokens_here // LEN
    heads_here = keys.shape[2] // HD
    group_size = QH // KVH
    prefix = prefix_keys.shape[1]
    stacked = jnp.concatenate([key_weight, value_weight], axis=2)
    query_list, input_list, key_list, value_list = ([], [], [], [])
    for layer_index in range(layer_count):
        split_shape = (seq_count, LEN, heads_here, group_size, HD)
        grad_query, token_key, token_value, prefix_key, prefix_value = attend_back(
            queries[layer_index].reshape(split_shape),
            keys[layer_index].reshape(seq_count, LEN, heads_here, HD),
            values[layer_index].reshape(seq_count, LEN, heads_here, HD),
            prefix_keys[layer_index].reshape(prefix, heads_here, HD),
            prefix_values[layer_index].reshape(prefix, heads_here, HD),
            dout[layer_index].reshape(split_shape),
        )
        query_list.append(grad_query.reshape(tokens_here, heads_here * group_size * HD))
        flat = jnp.concatenate(
            [
                token_key.reshape(tokens_here, heads_here * HD),
                token_value.reshape(tokens_here, heads_here * HD),
            ],
            axis=1,
        )
        partial_value = project_rows(
            flat, lax.all_gather(stacked[layer_index], "dp", axis=0, tiled=True)
        )
        input_list.append(
            lax.psum_scatter(
                partial_value.astype(jnp.bfloat16), "head", scatter_dimension=1, tiled=True
            )
        )
        prefix_key = prefix_key.reshape(prefix, heads_here * HD)
        prefix_value = prefix_value.reshape(prefix, heads_here * HD)
        prefix_key, prefix_value = lax.psum((prefix_key, prefix_value), "dp")
        key_list.append(prefix_key)
        value_list.append(prefix_value)
    key_grads = jnp.stack(key_list)
    value_grads = jnp.stack(value_list)
    return (jnp.stack(query_list), jnp.stack(input_list), key_grads, value_grads)


def solution(mesh):
    in_specs = (
        P(None, "dp", "head"),
        P(None, "dp", "head"),
        P(None, "dp", "head"),
        P(None, None, "head"),
        P(None, None, "head"),
        P(None, "dp", "head"),
        P(None, "dp", "head"),
        P(None, "dp", "head"),
    )
    out_specs = (
        P(None, "dp", "head"),
        P(None, "dp", "head"),
        P(None, None, "head"),
        P(None, None, "head"),
    )
    return jax.shard_map(shards, mesh=mesh, in_specs=in_specs, out_specs=out_specs, check_vma=False)
```

profile of v0, /device:TPU:1, one launch (start us, length us, event | category | flops | bytes accessed | tf_op | source)
XLA Modules:
  0.0 474.6 jit_solution(10344193172959845643)
XLA Ops:
  7.2 0.9 constant_dynamic-update-slice_fusion.1
  8.2 0.9 constant_dynamic-update-slice_fusion
  10.6 1.7 fusion.61
  13.8 0.9 fusion.66
  15.5 1.1 copy.117
  16.7 0.8 copy.55
  17.7 2.7 fusion.60
  20.4 2.3 copy.121
  22.8 1.1 fusion.12
  23.9 4.3 fusion.9
  28.2 1.3 fusion.11
  30.2 2.0 fusion.35
  32.2 0.8 copy.77
  33.6 1.9 fusion.63
  35.8 1.6 fusion.65
  37.7 4.9 %fusion.27 = f32[256,2,8]{0,2,1:T(8,128)S(1)} fusion(bf16[1,256,2,8,128]{1,4,3,2,0:T(8,128)(2,1)S(1)} %bitcast.255, bf16[1,256,2,128]{3,1,2,0:T(8,128)(2,1)S(1)} %copy.45, bf16[1,128,2,128]{3,1,2,0:T(8,128)(2,1)S(1)} %copy.44, f32[2,8,256]{2,1,0:T(8,128)} %get-tuple-element.4, f32[2,8,256]{2,1,0:T(8,128)S(1)} %get-tuple-element.24, ...), kind=kOutput, calls=%fused_computation.39 | convolution fusion | flops 412479488 | bytes 7684096 | tf_op jit(solution)/shard_map/bkgsm,bmkh->bskgh/dot_general | solution.py:30
  42.6 5.7 %fusion.14 = bf16[2,8,256,384]{2,3,1,0:T(8,128)(2,1)S(1)} fusion(f32[2,8,256]{2,1,0:T(8,128)S(1)} %bitcast.277, f32[2,8,256]{2,1,0:T(8,128)S(1)} %copy-done.19, f32[2,8,256]{2,1,0:T(8,128)S(1)} %get-tuple-element.24, f32[2,384,256,8]{2,1,3,0:T(8,128)} %copy-done.4, pred[256,384]{0,1:T(8,128)(4,1)S(1)} %iota_compare_fusion, ...), kind=kOutput, calls=%fused_computation.22 | convolution fusion | flops 415629312 | bytes 10829824 | tf_op jit(solution)/shard_map/bskgh,bmkh->bkgsm/dot_general | solution.py:34
  48.3 1.0 convolution_bitcast_fusion.1
  49.3 0.8 copy-done.7
  50.8 1.7 copy.74
  52.4 1.7 copy.120
  54.1 1.7 copy.61
  55.7 1.6 copy.119
  57.3 1.6 copy.60
  58.9 5.2 %fusion.26 = f32[256,2,8]{0,2,1:T(8,128)S(1)} fusion(bf16[1,256,2,8,128]{1,4,3,2,0:T(8,128)(2,1)} %bitcast.252, bf16[1,256,2,128]{3,1,2,0:T(8,128)(2,1)} %copy.61, bf16[1,128,2,128]{3,1,2,0:T(8,128)(2,1)} %copy.60, f32[2,8,256]{2,1,0:T(8,128)S(1)} %fusion.11, f32[2,8,256]{2,1,0:T(8,128)S(1)} %get-tuple-element.5, f32[2,384,256,8]{2,1,3,0:T(8,128)} %copy-done.3, ...), kind=kOutput, calls=%fused_computation.37 | convolution fusion | flops 412479488 | bytes 7684096 | tf_op jit(solution)/shard_map/bkgsm,bmkh->bskgh/dot_general | solution.py:30
  64.2 4.4 fusion.15
  68.6 1.7 copy-done
  70.3 1.0 convolution_bitcast_fusion
  72.8 1.7 copy.75
  74.5 5.0 %fusion.32 = f32[1,384,2,128]{1,3,2,0:T(8,128)S(1)} fusion(bf16[256,2,8,128]{0,3,2,1:T(8,128)(2,1)} %bitcast.257, f32[2,8,256]{2,1,0:T(8,128)} %get-tuple-element.4, f32[2,8,256]{2,1,0:T(8,128)S(1)} %get-tuple-element.24, f32[2,384,256,8]{2,1,3,0:T(8,128)} %copy-done.4, pred[256,384]{0,1:T(8,128)(4,1)S(1)} %iota_compare_fusion), kind=kOutput, calls=%fused_computation.42 | convolution fusion | flops 410517504 | bytes 7864320 | tf_op jit(solution)/shard_map/bkgsm,bskgh->bmkh/dot_general | solution.py:42
  80.9 1.7 copy.76
  82.8 1.6 slice.109
  84.4 1.6 slice.108
  86.1 12.0 %all-gather.5.cloned.1.call-done = bf16[1,8192,512]{2,1,0:T(8,128)(2,1)} async-done(((bf16[1,128,512]{2,1,0:T(8,128)(2,1)}), bf16[1,8192,512]{2,1,0:T(8,128)(2,1)}) %all-gather.5.cloned.1.call-update) | async-done | bytes 8388624 | tf_op jit(solution)/shard_map/all_gather | solution.py:88
  98.0 7.9 %convolution_convert_fusion.1 = bf16[256,8192]{1,0:T(8,128)(2,1)} fusion(bf16[1,8192,512]{2,1,0:T(8,128)(2,1)} %all-gather.5.cloned.1.call-done, bf16[256,256]{0,1:T(8,128)(2,1)} %bitcast.274, bf16[256,256]{0,1:T(8,128)(2,1)} %bitcast.272), kind=kOutput, calls=%fused_computation.1 | convolution fusion | flops 2150105088 | bytes 12845056 | tf_op jit(solution)/shard_map/dot_general | solution.py:55
  106.0 1.6 slice.106
  107.6 1.6 slice.107
  109.3 71.8 %all-gather.7.cloned.1.call-done = bf16[1,8192,512]{2,1,0:T(8,128)(2,1)} async-done(((bf16[1,128,512]{2,1,0:T(8,128)(2,1)}), bf16[1,8192,512]{2,1,0:T(8,128)(2,1)}) %all-gather.7.cloned.1.call-update) | async-done | bytes 8388624 | tf_op jit(solution)/shard_map/all_gather | solution.py:88
  181.0 7.9 %convolution_convert_fusion = bf16[256,8192]{1,0:T(8,128)(2,1)} fusion(bf16[1,8192,512]{2,1,0:T(8,128)(2,1)} %all-gather.7.cloned.1.call-done, bf16[256,256]{0,1:T(8,128)(2,1)} %bitcast.273, bf16[256,256]{0,1:T(8,128)(2,1)} %bitcast.275), kind=kOutput, calls=%fused_computation | convolution fusion | flops 2150105088 | bytes 12845056 | tf_op jit(solution)/shard_map/dot_general | solution.py:55
  188.9 1.7 convolution_convert_fusion.3
  190.7 1.5 copy.68
  192.2 2.8 convolution_convert_fusion.2
  195.6 1.5 pad_maximum_fusion
  197.1 165.4 %all-reduce.3.cloned.1.call-done = (f32[1,128,256]{2,1,0:T(8,128)}, f32[1,128,256]{2,1,0:T(8,128)}, f32[1,128,256]{2,1,0:T(8,128)}, f32[1,128,256]{2,1,0:T(8,128)}) async-done(((f32[1,128,256]{2,1,0:T(8,128)}, f32[1,128,256]{2,1,0:T(8,128)}, f32[1,128,256]{2,1,0:T(8,128)}, f32[1,128,256]{2,1,0:T(8,128)}), (f32[1,128,256]{2,1,0:T(8,128)}, f32[1,128,256]{2,1,0:T(8,128)}, f32[1,128,256]{2,1,0:T(8,128)}, ...) | async-done | bytes 524304 | tf_op jit(solution)/shard_map/psum | solution.py:97
  362.5 1.9 pad_maximum_fusion.2
  364.4 48.8 %reduce-scatter.3.cloned.1.call-done = bf16[256,2048]{1,0:T(8,128)(2,1)} async-done(((bf16[256,8192]{1,0:T(8,128)(2,1)}), bf16[256,2048]{1,0:T(8,128)(2,1)}) %reduce-scatter.3.cloned.1.call-update) | async-done | bytes 1048592 | tf_op jit(solution)/shard_map/reduce_scatter | solution.py:91
  413.3 51.7 %reduce-scatter.5.cloned.1.call-done = bf16[256,2048]{1,0:T(8,128)(2,1)} async-done(((bf16[256,8192]{1,0:T(8,128)(2,1)}), bf16[256,2048]{1,0:T(8,128)(2,1)}) %reduce-scatter.5.cloned.1.call-update) | async-done | bytes 1048592 | tf_op jit(solution)/shard_map/reduce_scatter | solution.py:91
  465.0 3.1 pad_maximum_fusion.1
  (70 shorter events, 10.5 us)
Async XLA Ops:
  7.2 5.7 %copy-start.12 = (bf16[2,256,256]{2,1,0:T(8,128)(2,1)S(1)}, bf16[2,256,256]{2,1,0:T(8,128)(2,1)}, u32[]{:S(2)}) copy-start(bf16[2,256,256]{2,1,0:T(8,128)(2,1)} %param.9) | copy-start | bytes 786436
  7.2 90.9 %all-gather.5.cloned.1.call-start = ((), (), s32[]{:S(2)}) async-start(), calls=%async_computation.4 | async-start | bytes 8519680 | tf_op jit(solution)/shard_map/all_gather | solution.py:88
  9.8 171.2 %all-gather.7.cloned.1.call-start = ((), (), s32[]{:S(2)}) async-start(), calls=%async_computation.5 | async-start | bytes 8519680 | tf_op jit(solution)/shard_map/all_gather | solution.py:88
  10.6 351.9 %all-reduce.3.cloned.1.call-start = ((), (), s32[]{:S(2)}) async-start(), calls=%async_computation.6 | async-start | bytes 1048576 | tf_op jit(solution)/shard_map/psum | solution.py:97
  12.9 11.0 %copy-start.1 = (bf16[1,256,2048]{1,2,0:T(8,128)(2,1)}, bf16[1,256,2048]{1,2,0:T(8,128)(2,1)S(1)}, u32[]{:S(2)}) copy-start(bf16[1,256,2048]{1,2,0:T(8,128)(2,1)S(1)} %copy.112) | copy-start | bytes 3145732
  15.5 8.4 %copy-start.5 = (bf16[1,256,2048]{1,2,0:T(8,128)(2,1)}, bf16[1,256,2048]{1,2,0:T(8,128)(2,1)S(1)}, u32[]{:S(2)}) copy-start(bf16[1,256,2048]{1,2,0:T(8,128)(2,1)S(1)} %copy.118) | copy-start | bytes 3145732
  23.9 4.3 copy-start.4
  28.2 4.0 copy-start.3
  28.2 2.0 copy-start.9
  32.1 0.8 copy-start.13
  33.6 8.9 %copy-start.11 = (bf16[1,256,2048]{1,2,0:T(8,128)(2,1)}, bf16[1,256,2048]{1,2,0:T(8,128)(2,1)S(1)}, u32[]{:S(2)}) copy-start(bf16[1,256,2048]{1,2,0:T(8,128)(2,1)S(1)} %copy.115) | copy-start | bytes 3145732
  35.8 6.7 %copy-start.16 = (bf16[1,256,2,128]{3,1,2,0:T(8,128)(2,1)}, bf16[1,256,2,128]{3,1,2,0:T(8,128)(2,1)S(1)}, u32[]{:S(2)}) copy-start(bf16[1,256,2,128]{3,1,2,0:T(8,128)(2,1)S(1)} %copy.45) | copy-start | bytes 393220
  37.6 4.9 %copy-start.18 = (bf16[1,128,2,128]{3,1,2,0:T(8,128)(2,1)}, bf16[1,128,2,128]{3,1,2,0:T(8,128)(2,1)S(1)}, u32[]{:S(2)}) copy-start(bf16[1,128,2,128]{3,1,2,0:T(8,128)(2,1)S(1)} %copy.44) | copy-start | bytes 196612
  37.6 4.9 %copy-start.19 = (f32[2,8,256]{2,1,0:T(8,128)S(1)}, f32[2,8,256]{2,1,0:T(8,128)}, u32[]{:S(2)}) copy-start(f32[2,8,256]{2,1,0:T(8,128)} %get-tuple-element.4) | copy-start | bytes 49156
  42.6 5.7 %copy-start.2 = (bf16[1,256,2048]{1,2,0:T(8,128)(2,1)S(1)}, bf16[1,256,2048]{1,2,0:T(8,128)(2,1)}, u32[]{:S(2)}) copy-start(bf16[1,256,2048]{1,2,0:T(8,128)(2,1)} %copy-done.1) | copy-start | bytes 3145732
  49.3 0.8 copy-start.7
  58.9 5.2 %copy-start.10 = (bf16[1,256,2048]{1,2,0:T(8,128)(2,1)S(1)}, bf16[1,256,2048]{1,2,0:T(8,128)(2,1)}, u32[]{:S(2)}) copy-start(bf16[1,256,2048]{1,2,0:T(8,128)(2,1)} %copy.121) | copy-start | bytes 3145732
  58.9 5.2 %copy-start.15 = (bf16[1,256,2,128]{3,1,2,0:T(8,128)(2,1)S(1)}, bf16[1,256,2,128]{3,1,2,0:T(8,128)(2,1)}, u32[]{:S(2)}) copy-start(bf16[1,256,2,128]{3,1,2,0:T(8,128)(2,1)} %copy.61) | copy-start | bytes 393220
  58.9 5.2 %copy-start.17 = (bf16[1,128,2,128]{3,1,2,0:T(8,128)(2,1)S(1)}, bf16[1,128,2,128]{3,1,2,0:T(8,128)(2,1)}, u32[]{:S(2)}) copy-start(bf16[1,128,2,128]{3,1,2,0:T(8,128)(2,1)} %copy.60) | copy-start | bytes 196612
  64.2 6.2 %copy-start.6 = (bf16[1,256,2048]{1,2,0:T(8,128)(2,1)S(1)}, bf16[1,256,2048]{1,2,0:T(8,128)(2,1)}, u32[]{:S(2)}) copy-start(bf16[1,256,2048]{1,2,0:T(8,128)(2,1)} %copy-done.5) | copy-start | bytes 3145732
  68.6 1.7 copy-start
  71.4 0.7 copy-start.8
  79.4 0.7 copy-start.14
  82.6 330.7 %reduce-scatter.3.cloned.1.call-start = ((), (), s32[]{:S(2)}) async-start(), calls=%async_computation.2 | async-start | bytes 5242880 | tf_op jit(solution)/shard_map/reduce_scatter | solution.py:91
  106.0 359.0 %reduce-scatter.5.cloned.1.call-start = ((), (), s32[]{:S(2)}) async-start(), calls=%async_computation.3 | async-start | bytes 5242880 | tf_op jit(solution)/shard_map/reduce_scatter | solution.py:91
Sparse Core Ops, SparseCore 0:
  10.8 87.2 all-gather.4
  100.8 80.1 all-gather.6
  184.9 177.5 all-reduce.2
  364.9 48.3 reduce-scatter.2
  415.8 49.1 reduce-scatter.4
where the time goes:
time: 476 us; the launch traced here: 475 us
  waiting for transfers between devices  350 us (74%)
  matrix products  54.9 us (12%)
  local copies, waits for them, and re-layouts  46.7 us (10%)
  between operations  14.2 us (3%)
  other arithmetic  7.9 us (2%)
    psum x1, waiting for transfers between devices, shards(): prefix_key, prefix_value = lax.psum((prefix_key, prefix_value), 'dp')  165 us
    reduce_scatter x2, waiting for transfers between devices, shards(): lax.psum_scatter(partial_value.astype(jnp.bfloat16), 'head', scatter_dime...  101 us
    all_gather x2, waiting for transfers between devices, shards(): lax.all_gather(stacked[layer_index], 'dp', axis=0, tiled=True)  83.7 us
    dot_general x2, matrix products, project_rows(): lax.dot_general(flat, weight_rows, (((1,), (1,)), ((), ())), preferred_el...  15.8 us
    unnamed x53, local copies, waits for them, and re-layouts  14.6 us
    dot_general x2, matrix products, attend_back(): jnp.einsum('bskgh,bmkh->bkgsm', dout, all_values, preferred_element_type=...  10.1 us
    dot_general x2, matrix products, attend_back(): jnp.einsum('bkgsm,bmkh->bskgh', probs_low, all_values, preferred_element_...  10.1 us
  transfers between devices with their start and end apart: 5, of which 5 were waited for; matrix products, arithmetic and copies ran while one was open for 21% of the time, Pallas kernels for 0%

commit v1 on v0

v1 whole, which is shorter than its diff:
```python
import functools

import jax
import jax.numpy as jnp
from jax import lax
from jax.experimental import pallas as pl
from jax.experimental.pallas import tpu as pltpu
from jax.sharding import Mesh
from jax.sharding import PartitionSpec as P

QH = 64
KVH = 8
HD = 128
LEN = 256
PREFIX = 128
GROUP = QH // KVH
SCALE = HD ** (-0.5)
VMEM_LIMIT = 48 * 1024 * 1024

NT = (((1,), (1,)), ((), ()))
NN = (((1,), (0,)), ((), ()))
TN = (((0,), (0,)), ((), ()))


def dot(a, b, dims):
    return lax.dot_general(a, b, dims, preferred_element_type=jnp.float32)


def attend_kernel(q_ref, k_ref, v_ref, pk_ref, pv_ref, do_ref, gq_ref, flat_ref, gpk_ref, gpv_ref):
    head = pl.program_id(1)
    all_keys = jnp.concatenate([pk_ref[0], k_ref[0]], axis=0)
    all_values = jnp.concatenate([pv_ref[0], v_ref[0]], axis=0)
    rows = PREFIX + LEN
    key_position = lax.broadcasted_iota(jnp.int32, (rows, LEN), 0) - PREFIX
    token_position = lax.broadcasted_iota(jnp.int32, (rows, LEN), 1)
    visible = key_position <= token_position
    key_terms = jnp.zeros((rows, HD), jnp.float32)
    value_terms = jnp.zeros((rows, HD), jnp.float32)
    for h in range(GROUP):
        cols = slice(h * HD, (h + 1) * HD)
        q = q_ref[0, :, cols]
        do = do_ref[0, :, cols]
        scores = dot(all_keys, q, NT) * SCALE
        scores = jnp.where(visible, scores, -1e30)
        peak = jnp.max(scores, axis=0, keepdims=True)
        exp_scores = jnp.exp(scores - peak)
        probs = exp_scores * (1.0 / jnp.sum(exp_scores, axis=0, keepdims=True))
        probs_low = probs.astype(jnp.bfloat16)
        dprobs = dot(all_values, do, NT)
        row_delta = jnp.sum(probs_low.astype(jnp.float32) * dprobs, axis=0, keepdims=True)
        dscores = (probs * (dprobs - row_delta) * SCALE).astype(jnp.bfloat16)
        gq_ref[0, :, cols] = dot(dscores, all_keys, TN).astype(jnp.bfloat16)
        key_terms += dot(dscores, q, NN)
        value_terms += dot(probs_low, do, NN)
    start = pl.multiple_of(head * HD, HD)
    flat_ref[0, :, pl.ds(start, HD)] = key_terms[PREFIX:].astype(jnp.bfloat16)
    start = pl.multiple_of((head + 2) * HD, HD)
    flat_ref[0, :, pl.ds(start, HD)] = value_terms[PREFIX:].astype(jnp.bfloat16)
    gpk_ref[0] = key_terms[:PREFIX]
    gpv_ref[0] = value_terms[:PREFIX]


def attend_back(queries, keys, values, prefix_keys, prefix_values, dout):
    layers = queries.shape[0]
    heads = keys.shape[2] // HD
    wide = pl.BlockSpec((1, LEN, GROUP * HD), lambda l, k: (l, 0, k))
    own = pl.BlockSpec((1, LEN, HD), lambda l, k: (l, 0, k))
    pre = pl.BlockSpec((1, PREFIX, HD), lambda l, k: (l, 0, k))
    flat = pl.BlockSpec((1, LEN, 2 * heads * HD), lambda l, k: (l, 0, 0))
    return pl.pallas_call(
        attend_kernel,
        grid=(layers, heads),
        in_specs=[wide, own, own, pre, pre, wide],
        out_specs=[wide, flat, pre, pre],
        out_shape=[
            jax.ShapeDtypeStruct(queries.shape, jnp.bfloat16),
            jax.ShapeDtypeStruct((layers, LEN, 2 * heads * HD), jnp.bfloat16),
            jax.ShapeDtypeStruct((layers, PREFIX, heads * HD), jnp.float32),
            jax.ShapeDtypeStruct((layers, PREFIX, heads * HD), jnp.float32),
        ],
        compiler_params=pltpu.CompilerParams(vmem_limit_bytes=VMEM_LIMIT),
        cost_estimate=pl.CostEstimate(
            flops=5 * 2 * layers * heads * GROUP * LEN * (PREFIX + LEN) * HD,
            bytes_accessed=8 * 1024 * 1024,
            transcendentals=layers * heads * GROUP * LEN * (PREFIX + LEN),
        ),
    )(queries, keys, values, prefix_keys, prefix_values, dout)


def project_kernel(y_ref, *refs):
    (f0, f1, f2, f3, g0, g1, g2, g3, w0, w1, w2, w3, mine_ref, other_ref) = refs
    total = [None, None]
    for side, group in enumerate(((f0, f1, f2, f3), (g0, g1, g2, g3))):
        acc = None
        for f, w in zip(group, (w0, w1, w2, w3)):
            rows = w[0, :, 0].reshape(-1, w.shape[-1])
            term = dot(f[0], rows, NT)
            acc = term if acc is None else acc + term
        total[side] = acc.astype(jnp.bfloat16)
    mine_ref[0] = total[0]
    other_ref[0] = total[1]


def project(own, other, weights, y):
    layers, tokens, width = own[0].shape
    y_count, z_count, _, rows, _ = weights.shape
    step = 2
    flat_spec = pl.BlockSpec((1, tokens, width), lambda l, n, y_ref: (l, 0, 0))

    def weight_spec(shift):
        return pl.BlockSpec(
            (1, step, 1, rows, width),
            lambda l, n, y_ref: (lax.rem(y_ref[0] + (y_count - shift), y_count), n, l, 0, 0),
        )

    out_spec = pl.BlockSpec((1, tokens, step * rows), lambda l, n, y_ref: (l, 0, n))
    out_type = jax.ShapeDtypeStruct((layers, tokens, z_count * rows), jnp.bfloat16)
    return pl.pallas_call(
        project_kernel,
        grid_spec=pltpu.PrefetchScalarGridSpec(
            num_scalar_prefetch=1,
            grid=(layers, z_count // step),
            in_specs=[flat_spec] * 8 + [weight_spec(s) for s in range(4)],
            out_specs=[out_spec, out_spec],
        ),
        out_shape=[out_type, out_type],
        compiler_params=pltpu.CompilerParams(vmem_limit_bytes=VMEM_LIMIT),
        cost_estimate=pl.CostEstimate(
            flops=2 * layers * 2 * tokens * z_count * rows * y_count * width,
            bytes_accessed=14 * 1024 * 1024,
            transcendentals=0,
        ),
    )(y, *own, *other, weights, weights, weights, weights)


def weave_kernel(core_ref, mine_ref, theirs_ref, out_ref):
    mine = mine_ref[0]
    theirs = theirs_ref[0]
    first = core_ref[0] == 0
    rows = 128
    for j in range(mine.shape[1] // rows):
        cols = slice(j * rows, (j + 1) * rows)
        a = mine[:, cols]
        b = theirs[:, cols]
        out_ref[0, :, 2 * j * rows : (2 * j + 1) * rows] = jnp.where(first, a, b)
        out_ref[0, :, (2 * j + 1) * rows : (2 * j + 2) * rows] = jnp.where(first, b, a)


def weave(mine, theirs, core):
    layers, tokens, width = mine.shape
    step = 512
    part = pl.BlockSpec((1, tokens, step), lambda l, n, c: (l, 0, n))
    return pl.pallas_call(
        weave_kernel,
        grid_spec=pltpu.PrefetchScalarGridSpec(
            num_scalar_prefetch=1,
            grid=(layers, width // step),
            in_specs=[part, part],
            out_specs=pl.BlockSpec((1, tokens, 2 * step), lambda l, n, c: (l, 0, n)),
        ),
        out_shape=jax.ShapeDtypeStruct((layers, tokens, 2 * width), jnp.bfloat16),
        compiler_params=pltpu.CompilerParams(vmem_limit_bytes=VMEM_LIMIT),
    )(core, mine, theirs)


def ring(count, shift):
    return [(i, (i + shift) % count) for i in range(count)]


def swap_cores(a):
    return lax.ppermute(a, "core", [(0, 1), (1, 0)])


def sum_prefix(gpk, gpv, core, replicas):
    layers, rows, width = gpk.shape
    keep = jnp.where(core == 0, gpk, gpv)
    send = jnp.where(core == 0, gpv, gpk)
    half = (keep + swap_cores(send)).reshape(layers * rows, width)
    pieces = lax.all_to_all(half, ("x", "z"), 0, 0, tiled=True)
    piece = jnp.sum(pieces.reshape(replicas, -1, width), axis=0)
    spread = jnp.broadcast_to(piece[None], (replicas,) + piece.shape).reshape(-1, width)
    whole = lax.all_to_all(spread, ("x", "z"), 0, 0, tiled=True).reshape(layers, rows, width)
    theirs = swap_cores(whole)
    return jnp.where(core == 0, whole, theirs), jnp.where(core == 0, theirs, whole)


def shards(queries, keys, values, prefix_keys, prefix_values, dout, key_weight, value_weight):
    y = lax.axis_index("y").reshape(1).astype(jnp.int32)
    core = lax.axis_index("core")
    stacked = jnp.concatenate([key_weight, value_weight], axis=2)
    turned = lax.ppermute(
        stacked, ("x", "y"), [(i * 4 + j, j * 4 + i) for i in range(4) for j in range(4)]
    )
    weights = lax.all_gather(turned, ("x", "z"), axis=0)
    weights = weights.reshape((4, 8) + turned.shape)
    grad_queries, flat, gpk, gpv = attend_back(
        queries, keys, values, prefix_keys, prefix_values, dout
    )
    own = [flat] + [lax.ppermute(flat, "y", ring(4, s)) for s in (1, 2, 3)]
    other = [swap_cores(a) for a in own]
    grad_prefix_keys, grad_prefix_values = sum_prefix(gpk, gpv, core, 32)
    mine, give = project(own, other, weights, y)
    theirs = swap_cores(give)
    grad_input = weave(mine, theirs, core.reshape(1).astype(jnp.int32))
    return grad_queries, grad_input, grad_prefix_keys, grad_prefix_values


def solution(mesh):
    mesh = Mesh(mesh.devices.reshape(4, 8, 2, 4), ("x", "z", "core", "y"))
    dp = ("x", "z", "core")
    split = P(None, dp, "y")
    shared = P(None, None, "y")
    in_specs = (split, split, split, shared, shared, split, split, split)
    out_specs = (split, split, shared, shared)
    return jax.shard_map(shards, mesh=mesh, in_specs=in_specs, out_specs=out_specs, check_vma=False)
```

time: 476 us -> 175 us (0.37)
  waiting for transfers between devices: 350 us -> 60.9 us
  matrix products: 54.9 us -> 0 us
  starting transfers between devices: 0.42 us -> 38 us
  local copies, waits for them, and re-layouts: 46.7 us -> 9.43 us
  Pallas kernels: 0 us -> 32.4 us
  blocking collectives: 0 us -> 16.4 us
  other arithmetic: 7.9 us -> 2.65 us
    psum x1 -> x0, waiting for transfers between devices: 165 us -> none  [shards(): prefix_key, prefix_value = lax.psum((prefix_key, prefix_value), 'dp')]
    reduce_scatter x2 -> x0, waiting for transfers between devices: 101 us -> none  [shards(): lax.psum_scatter(partial_value.astype(jnp.bfloat16), 'head', scatter_dime...]
    dot_general x14 -> x0, matrix products: 54.9 us -> none  [the longest x2 15.8 us: project_rows(): lax.dot_general(flat, weight_rows, (((1,), (1,)), ((), ())), preferred_el...]
    all_gather x2 -> x1, waiting for transfers between devices: 83.7 us -> 37.4 us  [shards(): weights = lax.all_gather(turned, ('x', 'z'), axis=0)]
    pallas_call x0 -> x3, Pallas kernels: none -> 32.4 us  [the longest x1 20.2 us: attend_back(): pl.pallas_call(attend_kernel, grid=(layers, heads), in_specs=[wide, own,...]
    ppermute x0 -> x11, starting transfers between devices: none -> 29.3 us  [the longest x3 22 us: shards(): own = [flat] + [lax.ppermute(flat, 'y', ring(4, s)) for s in (1, 2, 3)]]
    ppermute x0 -> x11, waiting for transfers between devices: none -> 23.5 us  [the longest x3 22.3 us: shards(): own = [flat] + [lax.ppermute(flat, 'y', ring(4, s)) for s in (1, 2, 3)]]
    slice x15 -> x0, local copies, waits for them, and re-layouts: 18.7 us -> none  [the longest x2 3.24 us: attend_back(): key_terms[:, prefix:].astype(jnp.bfloat16)]
  transfers between devices with their start and end apart: 5 -> 13, of which waited for: 5 -> 4; matrix products, arithmetic and copies ran while one was open for 21% -> 1% of each run, Pallas kernels for 0% -> 17%
where the time goes in v1:
time: 175 us; the launch traced here: 174 us
  waiting for transfers between devices  60.9 us (35%)
  starting transfers between devices  38 us (22%)
  Pallas kernels  32.4 us (19%)
  blocking collectives  16.4 us (9%)
  between operations  14.1 us (8%)
  local copies, waits for them, and re-layouts  9.43 us (5%)
  other arithmetic  2.65 us (2%)
    all_gather x1, waiting for transfers between devices, shards(): weights = lax.all_gather(turned, ('x', 'z'), axis=0)  37.4 us
    ppermute x3, waiting for transfers between devices, shards(): own = [flat] + [lax.ppermute(flat, 'y', ring(4, s)) for s in (1, 2, 3)]  22.3 us
    ppermute x3, starting transfers between devices, shards(): own = [flat] + [lax.ppermute(flat, 'y', ring(4, s)) for s in (1, 2, 3)]  22 us
    pallas_call x1, Pallas kernels, attend_back(): pl.pallas_call(attend_kernel, grid=(layers, heads), in_specs=[wide, own,...  20.2 us
    all_to_all x1, blocking collectives, sum_prefix(): lax.all_to_all(spread, ('x', 'z'), 0, 0, tiled=True)  16.4 us
    pallas_call x1, Pallas kernels, project(): pl.pallas_call(project_kernel, grid_spec=pltpu.PrefetchScalarGridSpec(num...  10.1 us
    unnamed x18, local copies, waits for them, and re-layouts  9.41 us
    all_to_all x1, starting transfers between devices, sum_prefix(): pieces = lax.all_to_all(half, ('x', 'z'), 0, 0, tiled=True)  8.57 us
  transfers between devices with their start and end apart: 13, of which 4 were waited for; matrix products, arithmetic and copies ran while one was open for 1% of the time, Pallas kernels for 17%

profile of v1, /device:TPU:1, one launch (start us, length us, event | category | flops | bytes accessed | tf_op | source)
XLA Modules:
  0.0 173.9 jit_solution(2706435766420448094)
XLA Ops:
  7.2 0.0 all-gather.3.cloned.1.call-start
  7.2 1.0 pad_maximum_fusion
  8.2 0.7 collective-permute-start.7
  8.9 0.0 collective-permute-done.7
  8.9 0.0 copy-start.8
  8.9 0.7 copy-done.8
  9.6 0.0 all-gather.3.cloned.1.call-update
  9.6 0.0 copy-start.2
  9.6 1.6 copy-done.2
  11.2 0.0 copy-start.3
  11.2 1.6 copy-done.3
  12.8 0.0 copy-start.4
  12.8 0.9 copy-done.4
  13.8 0.9 copy-done.5
  14.7 0.9 copy-done.6
  15.6 0.9 copy-done.7
  16.5 20.2 %shard_map.111 = (bf16[2,256,2048]{2,1,0:T(8,128)(2,1)}, bf16[2,256,512]{2,1,0:T(8,128)(2,1)S(1)}, f32[2,128,256]{2,1,0:T(8,128)S(1)}, f32[2,128,256]{2,1,0:T(8,128)S(1)}) custom-call(bf16[2,256,2048]{2,1,0:T(8,128)(2,1)S(1)} %copy-done.2, bf16[2,256,256]{2,1,0:T(8,128)(2,1)S(1)} %copy-done.4, bf16[2,256,256]{2,1,0:T(8,128)(2,1)S(1)} %copy-done.5, ...), custom_call_target="tpu_custom_call" | custom-call | flops 4026531840 | bytes 8388608 | tf_op jit(solution)/shard_map/pallas_call | solution.py:70
  36.7 21.4 %collective-permute-start.2 = (bf16[2,256,512]{2,1,0:T(8,128)(2,1)S(1)}, bf16[2,256,512]{2,1,0:T(8,128)(2,1)S(1)}, u32[]{:S(2)}, u32[]{:S(2)}) collective-permute-start(bf16[2,256,512]{2,1,0:T(8,128)(2,1)S(1)} %get-tuple-element.11.refs_0_), channel_id=1, source_target_pairs={{0,3},{1,0},{2,1},{3,2},{4,7},{5,4},{6,5},{7,6},{8,11},{9,8},{10,9... | collective-permute-start | bytes 1572872 | tf_op jit(solution)/shard_map/ppermute | solution.py:199
  58.1 0.0 collective-permute-start.1
  58.1 0.6 collective-permute-start
  58.7 1.6 collective-permute-start.9
  60.4 0.1 collective-permute-start.3
  60.5 19.7 %collective-permute-done.2.refs_3_ = bf16[2,256,512]{2,1,0:T(8,128)(2,1)S(1)} collective-permute-done((bf16[2,256,512]{2,1,0:T(8,128)(2,1)S(1)}, bf16[2,256,512]{2,1,0:T(8,128)(2,1)S(1)}, u32[]{:S(2)}, u32[]{:S(2)}) %collective-permute-start.2) | collective-permute-done | bytes 524320 | tf_op jit(solution)/shard_map/ppermute | solution.py:199
  80.1 1.4 collective-permute-start.6
  81.5 0.0 collective-permute-done.1.refs_2_
  81.5 0.0 collective-permute-start.5
  81.5 2.7 %collective-permute-done.refs_1_ = bf16[2,256,512]{2,1,0:T(8,128)(2,1)S(1)} collective-permute-done((bf16[2,256,512]{2,1,0:T(8,128)(2,1)S(1)}, bf16[2,256,512]{2,1,0:T(8,128)(2,1)S(1)}, u32[]{:S(2)}, u32[]{:S(2)}) %collective-permute-start) | collective-permute-done | bytes 524320 | tf_op jit(solution)/shard_map/ppermute | solution.py:199
  84.2 0.7 collective-permute-start.4
  84.9 0.0 collective-permute-done.9
  84.9 0.8 select_add_fusion
  85.7 8.6 %all-to-all-start = ((f32[32,8,256]{2,1,0:T(8,128)}), f32[32,8,256]{2,1,0:T(8,128)S(1)}, u32[]{:S(2)}, u32[]{:S(2)}) async-start(f32[32,8,256]{2,1,0:T(8,128)} %bitcast.12), calls=%async_computation | async-start | bytes 524288 | tf_op jit(solution)/shard_map/all_to_all | solution.py:179
  94.3 0.0 collective-permute-done.3.refs_4_
  94.3 0.0 copy-start
  94.3 0.8 copy-done
  95.1 0.0 collective-permute-done.6.refs_7_
  95.1 0.0 collective-permute-done.5.refs_6_
  95.1 0.0 collective-permute-done.4.refs_5_
  95.1 37.4 %all-gather.3.cloned.1.call-done = bf16[64,128,512]{2,1,0:T(8,128)(2,1)} async-done(((bf16[2,128,512]{2,1,0:T(8,128)(2,1)}), bf16[64,128,512]{2,1,0:T(8,128)(2,1)}) %all-gather.3.cloned.1.call-update) | async-done | bytes 8388624 | tf_op jit(solution)/shard_map/all_gather | solution.py:194
  132.5 1.0 copy-done.1
  133.5 10.1 %shard_map.112 = (bf16[2,256,1024]{2,1,0:T(8,128)(2,1)S(1)}, bf16[2,256,1024]{2,1,0:T(8,128)(2,1)}) custom-call(s32[1]{0:T(128)} %bitcast.1.y_ref, bf16[2,256,512]{2,1,0:T(8,128)(2,1)S(1)} %get-tuple-element.11.refs_0_, bf16[2,256,512]{2,1,0:T(8,128)(2,1)S(1)} %collective-permute-done.refs_1_, bf16[2,256,512]{2,1,0:T(8,128)(2,1)S(1)} %collective-permute-done.1.refs_2_, ...), custom_call_target="tpu_custom_call" | custom-call | flops 4294967296 | bytes 14680064 | tf_op jit(solution)/shard_map/pallas_call | solution.py:118
  143.6 0.5 collective-permute-start.8
  144.1 0.0 all-to-all-done
  144.1 16.4 %all_to_all.15 = f32[32,8,256]{2,1,0:T(8,128)S(1)} all-to-all(f32[32,8,256]{2,1,0:T(8,128)S(1)} %broadcast_in_dim.2), channel_id=1, replica_groups=mesh['x'=4,'z'=8,'core'=2,'y'=4] {'x','z'}, dimensions={0} | all-to-all | bytes 524288 | tf_op jit(solution)/shard_map/all_to_all | solution.py:182
  160.6 2.3 %collective-permute-start.10 = (f32[2,128,256]{2,1,0:T(8,128)S(1)}, f32[2,128,256]{2,1,0:T(8,128)S(1)}, u32[]{:S(2)}, u32[]{:S(2)}) collective-permute-start(f32[2,128,256]{2,1,0:T(8,128)S(1)} %bitcast.13), channel_id=1, source_target_pairs={{0,4},{4,0},{1,5},{5,1},{2,6},{6,2},{3,7},{7,3},{8,12},{12,8},{9,1... | collective-permute-start | bytes 786440 | tf_op jit(solution)/shard_map/ppermute | solution.py:171
  162.9 1.2 collective-permute-done.10
  164.1 0.8 broadcast_select_fusion
  164.9 0.0 collective-permute-done.8.theirs_ref
  164.9 2.2 %shard_map.113 = bf16[2,256,2048]{2,1,0:T(8,128)(2,1)} custom-call(s32[1]{0:T(128)} %bitcast.core_ref, bf16[2,256,1024]{2,1,0:T(8,128)(2,1)S(1)} %get-tuple-element.12.mine_ref, bf16[2,256,1024]{2,1,0:T(8,128)(2,1)S(1)} %collective-permute-done.8.theirs_ref), custom_call_target="tpu_custom_call" | custom-call | tf_op jit(solution)/shard_map/pallas_call | solution.py:153
  (7 shorter events, 0.1 us)
Async XLA Ops:
  7.2 125.3 %all-gather.3.cloned.1.call-start = ((), (), s32[]{:S(2)}) async-start(), calls=%async_computation.2 | async-start | bytes 8650752 | tf_op jit(solution)/shard_map/all_gather | solution.py:194
  8.2 0.7 collective-permute-start.7
  8.9 0.7 copy-start.8
  9.6 1.6 copy-start.2
  11.2 1.6 copy-start.3
  12.8 0.9 copy-start.4
  13.8 0.9 copy-start.5
  14.7 0.9 copy-start.6
  15.6 0.9 copy-start.7
  36.7 43.4 %collective-permute-start.2 = (bf16[2,256,512]{2,1,0:T(8,128)(2,1)S(1)}, bf16[2,256,512]{2,1,0:T(8,128)(2,1)S(1)}, u32[]{:S(2)}, u32[]{:S(2)}) collective-permute-start(bf16[2,256,512]{2,1,0:T(8,128)(2,1)S(1)} %get-tuple-element.11.refs_0_), channel_id=1, source_target_pairs={{0,3},{1,0},{2,1},{3,2},{4,7},{5,4},{6,5},{7,6},{8,11},{9,8},{10,9... | collective-permute-start | bytes 1572872 | tf_op jit(solution)/shard_map/ppermute | solution.py:199
  58.1 23.4 %collective-permute-start.1 = (bf16[2,256,512]{2,1,0:T(8,128)(2,1)S(1)}, bf16[2,256,512]{2,1,0:T(8,128)(2,1)S(1)}, u32[]{:S(2)}, u32[]{:S(2)}) collective-permute-start(bf16[2,256,512]{2,1,0:T(8,128)(2,1)S(1)} %get-tuple-element.11.refs_0_), channel_id=1, source_target_pairs={{0,2},{1,3},{2,0},{3,1},{4,6},{5,7},{6,4},{7,5},{8,10},{9,11},{10,... | collective-permute-start | bytes 1572872 | tf_op jit(solution)/shard_map/ppermute | solution.py:199
  58.1 26.0 %collective-permute-start = (bf16[2,256,512]{2,1,0:T(8,128)(2,1)S(1)}, bf16[2,256,512]{2,1,0:T(8,128)(2,1)S(1)}, u32[]{:S(2)}, u32[]{:S(2)}) collective-permute-start(bf16[2,256,512]{2,1,0:T(8,128)(2,1)S(1)} %get-tuple-element.11.refs_0_), channel_id=1, source_target_pairs={{0,1},{1,2},{2,3},{3,0},{4,5},{5,6},{6,7},{7,4},{8,9},{9,10},{10,1... | collective-permute-start | bytes 1572872 | tf_op jit(solution)/shard_map/ppermute | solution.py:199
  58.7 26.2 %collective-permute-start.9 = (f32[2,128,256]{2,1,0:T(8,128)S(1)}, f32[2,128,256]{2,1,0:T(8,128)S(1)}, u32[]{:S(2)}, u32[]{:S(2)}) collective-permute-start(f32[2,128,256]{2,1,0:T(8,128)S(1)} %broadcast_select_fusion.2), channel_id=1, source_target_pairs={{0,4},{4,0},{1,5},{5,1},{2,6},{6,2},{3,7},{7,3},{8,12},{12,8},{9,1... | collective-permute-start | bytes 786440 | tf_op jit(solution)/shard_map/ppermute | solution.py:171
  60.4 33.9 %collective-permute-start.3 = (bf16[2,256,512]{2,1,0:T(8,128)(2,1)S(1)}, bf16[2,256,512]{2,1,0:T(8,128)(2,1)S(1)}, u32[]{:S(2)}, u32[]{:S(2)}) collective-permute-start(bf16[2,256,512]{2,1,0:T(8,128)(2,1)S(1)} %get-tuple-element.11.refs_0_), channel_id=1, source_target_pairs={{0,4},{4,0},{1,5},{5,1},{2,6},{6,2},{3,7},{7,3},{8,12},{12,8},{9,1... | collective-permute-start | bytes 1572872 | tf_op jit(solution)/shard_map/ppermute | solution.py:171
  80.1 14.9 %collective-permute-start.6 = (bf16[2,256,512]{2,1,0:T(8,128)(2,1)S(1)}, bf16[2,256,512]{2,1,0:T(8,128)(2,1)}, u32[]{:S(2)}, u32[]{:S(2)}) collective-permute-start(bf16[2,256,512]{2,1,0:T(8,128)(2,1)S(1)} %collective-permute-done.2.refs_3_), channel_id=1, source_target_pairs={{0,4},{4,0},{1,5},{5,1},{2,6},{6,2},{3,7},{7,3},{8,12},{12,8},{9,1... | collective-permute-start | bytes 1572872 | tf_op jit(solution)/shard_map/ppermute | solution.py:171
  81.5 13.6 %collective-permute-start.5 = (bf16[2,256,512]{2,1,0:T(8,128)(2,1)S(1)}, bf16[2,256,512]{2,1,0:T(8,128)(2,1)}, u32[]{:S(2)}, u32[]{:S(2)}) collective-permute-start(bf16[2,256,512]{2,1,0:T(8,128)(2,1)S(1)} %collective-permute-done.1.refs_2_), channel_id=1, source_target_pairs={{0,4},{4,0},{1,5},{5,1},{2,6},{6,2},{3,7},{7,3},{8,12},{12,8},{9,1... | collective-permute-start | bytes 1572872 | tf_op jit(solution)/shard_map/ppermute | solution.py:171
  84.2 10.9 %collective-permute-start.4 = (bf16[2,256,512]{2,1,0:T(8,128)(2,1)S(1)}, bf16[2,256,512]{2,1,0:T(8,128)(2,1)}, u32[]{:S(2)}, u32[]{:S(2)}) collective-permute-start(bf16[2,256,512]{2,1,0:T(8,128)(2,1)S(1)} %collective-permute-done.refs_1_), channel_id=1, source_target_pairs={{0,4},{4,0},{1,5},{5,1},{2,6},{6,2},{3,7},{7,3},{8,12},{12,8},{9,1... | collective-permute-start | bytes 1572872 | tf_op jit(solution)/shard_map/ppermute | solution.py:171
  85.7 58.4 %all-to-all-start = ((f32[32,8,256]{2,1,0:T(8,128)}), f32[32,8,256]{2,1,0:T(8,128)S(1)}, u32[]{:S(2)}, u32[]{:S(2)}) async-start(f32[32,8,256]{2,1,0:T(8,128)} %bitcast.12), calls=%async_computation | async-start | bytes 524288 | tf_op jit(solution)/shard_map/all_to_all | solution.py:179
  94.3 0.8 copy-start
  132.5 1.0 copy-start.1
  143.6 21.3 %collective-permute-start.8 = (bf16[2,256,1024]{2,1,0:T(8,128)(2,1)}, bf16[2,256,1024]{2,1,0:T(8,128)(2,1)S(1)}, u32[]{:S(2)}, u32[]{:S(2)}) collective-permute-start(bf16[2,256,1024]{2,1,0:T(8,128)(2,1)} %get-tuple-element.13), channel_id=1, source_target_pairs={{0,4},{4,0},{1,5},{5,1},{2,6},{6,2},{3,7},{7,3},{8,12},{12,8},{9,1... | collective-permute-start | bytes 3145736 | tf_op jit(solution)/shard_map/ppermute | solution.py:171
  160.6 3.5 %collective-permute-start.10 = (f32[2,128,256]{2,1,0:T(8,128)S(1)}, f32[2,128,256]{2,1,0:T(8,128)S(1)}, u32[]{:S(2)}, u32[]{:S(2)}) collective-permute-start(f32[2,128,256]{2,1,0:T(8,128)S(1)} %bitcast.13), channel_id=1, source_target_pairs={{0,4},{4,0},{1,5},{5,1},{2,6},{6,2},{3,7},{7,3},{8,12},{12,8},{9,1... | collective-permute-start | bytes 786440 | tf_op jit(solution)/shard_map/ppermute | solution.py:171
Sparse Core Ops, SparseCore 0:
  11.2 121.2 all-gather.2

commit v2 on v1

v2 whole, which is shorter than its diff:
```python
import functools
import math

import jax
import jax.numpy as jnp
from jax import lax
from jax.experimental import pallas as pl
from jax.experimental.pallas import tpu as pltpu
from jax.sharding import Mesh
from jax.sharding import PartitionSpec as P

QH = 64
KVH = 8
HD = 128
LEN = 256
PREFIX = 128
GROUP = QH // KVH
SCALE = HD ** (-0.5)
VMEM_LIMIT = 60 * 1024 * 1024
EXP2 = SCALE * math.log2(math.e)
COST = pl.CostEstimate(flops=2 * 10**9, bytes_accessed=16 * 10**6, transcendentals=0)
BRIEF = pl.CostEstimate(flops=1, bytes_accessed=1, transcendentals=0)

NT = (((1,), (1,)), ((), ()))
NN = (((1,), (0,)), ((), ()))
TN = (((0,), (0,)), ((), ()))


def dot(a, b, dims):
    return lax.dot_general(a, b, dims, preferred_element_type=jnp.float32)


def attend_kernel(q_ref, k_ref, v_ref, pk_ref, pv_ref, do_ref, gq_ref, flat_ref, terms_ref):
    half = LEN // 2
    keys = jnp.concatenate([pk_ref[0], k_ref[0]], axis=0)
    values = jnp.concatenate([pv_ref[0], v_ref[0]], axis=0)
    key_row = lax.broadcasted_iota(jnp.int32, (half, 2 * half), 0)
    token = lax.rem(lax.broadcasted_iota(jnp.int32, (half, 2 * half), 1), half)
    visible = key_row <= token
    key_terms = [0.0, 0.0]
    value_terms = [0.0, 0.0]
    for pair in range(GROUP // 2):
        for part in range(2):
            rows = PREFIX + (part + 1) * half
            tokens = slice(part * half, (part + 1) * half)
            columns = [slice((2 * pair + i) * HD, (2 * pair + i + 1) * HD) for i in range(2)]
            q = jnp.concatenate([q_ref[0, tokens, c] for c in columns], axis=0)
            do = jnp.concatenate([do_ref[0, tokens, c] for c in columns], axis=0)
            scores = dot(keys[:rows], q, NT)
            last = jnp.where(visible, scores[rows - half :], -1e30)
            scores = jnp.concatenate([scores[: rows - half], last], axis=0)
            peak = jnp.max(scores, axis=0, keepdims=True)
            exp_scores = jnp.exp2((scores - peak) * EXP2)
            probs = exp_scores * (1.0 / jnp.sum(exp_scores, axis=0, keepdims=True))
            dprobs = dot(values[:rows], do, NT)
            row_delta = jnp.sum(probs * dprobs, axis=0, keepdims=True)
            dscores = (probs * (dprobs - row_delta)).astype(jnp.bfloat16)
            gq = (dot(dscores, keys[:rows], TN) * SCALE).astype(jnp.bfloat16)
            for i, c in enumerate(columns):
                gq_ref[0, tokens, c] = gq[i * half : (i + 1) * half]
            key_terms[part] += dot(dscores, q, NN)
            value_terms[part] += dot(probs.astype(jnp.bfloat16), do, NN)
    split = PREFIX + half
    for i, (terms, scale) in enumerate(((key_terms, SCALE), (value_terms, 1.0))):
        low = (terms[0] + terms[1][:split]) * scale
        high = terms[1][split:] * scale
        flat_ref[0, :half, i * HD : (i + 1) * HD] = low[PREFIX:].astype(jnp.bfloat16)
        flat_ref[0, half:, i * HD : (i + 1) * HD] = high.astype(jnp.bfloat16)
        terms_ref[i, 0] = low[:PREFIX]


def attend_back(queries, keys, values, prefix_keys, prefix_values, dout):
    layers, _, width = keys.shape
    heads = width // HD
    wide = pl.BlockSpec((1, LEN, GROUP * HD), lambda l, h: (l, 0, h))
    own = pl.BlockSpec((1, LEN, HD), lambda l, h: (l, 0, h))
    pre = pl.BlockSpec((1, PREFIX, HD), lambda l, h: (l, 0, h))
    flat = pl.BlockSpec((1, LEN, 2 * HD), lambda l, h: (l, 0, h))
    terms = pl.BlockSpec((2, 1, PREFIX, HD), lambda l, h: (0, l, 0, h))
    return pl.pallas_call(
        attend_kernel,
        grid=(layers, heads),
        in_specs=[wide, own, own, pre, pre, wide],
        out_specs=[wide, flat, terms],
        out_shape=[
            jax.ShapeDtypeStruct(queries.shape, jnp.bfloat16),
            jax.ShapeDtypeStruct((layers, LEN, 2 * width), jnp.bfloat16),
            jax.ShapeDtypeStruct((2, layers, PREFIX, width), jnp.float32),
        ],
        compiler_params=pltpu.CompilerParams(vmem_limit_bytes=VMEM_LIMIT),
        cost_estimate=COST,
    )(queries, keys, values, prefix_keys, prefix_values, dout)


def project_kernel(y_ref, f0, f1, f2, f3, w0, w1, w2, w3, out_ref):
    total = None
    for f, w in zip((f0, f1, f2, f3), (w0, w1, w2, w3)):
        term = dot(f[0], w[...].reshape(-1, w.shape[-1]), NT)
        total = term if total is None else total + term
    out_ref[0] = total.astype(jnp.bfloat16)


def project(flats, weights, y):
    layers, tokens, depth = flats[0].shape
    rows = weights.shape[4]
    step = 2
    flat_spec = pl.BlockSpec((1, tokens, depth), lambda l, n, y_ref: (l, 0, 0))

    def weight_spec(shift):
        return pl.BlockSpec(
            (1, step, 2, 1, rows, depth),
            lambda l, n, y_ref: (lax.rem(y_ref[0] + 4 - shift, 4), n, 0, l, 0, 0),
        )

    return pl.pallas_call(
        project_kernel,
        grid_spec=pltpu.PrefetchScalarGridSpec(
            num_scalar_prefetch=1,
            grid=(layers, 8 // step),
            in_specs=[flat_spec] * 4 + [weight_spec(s) for s in range(4)],
            out_specs=pl.BlockSpec((1, tokens, step * 2 * rows), lambda l, n, y_ref: (l, 0, n)),
        ),
        out_shape=jax.ShapeDtypeStruct((layers, tokens, 16 * rows), jnp.bfloat16),
        compiler_params=pltpu.CompilerParams(vmem_limit_bytes=VMEM_LIMIT),
        cost_estimate=COST,
    )(y, *flats, weights, weights, weights, weights)


def gate_kernel(*refs):
    pass


def gate(*arrays):
    anywhere = [pl.BlockSpec(memory_space=pl.ANY)] * len(arrays)
    return pl.pallas_call(
        gate_kernel,
        in_specs=anywhere,
        out_specs=anywhere,
        out_shape=[jax.ShapeDtypeStruct(a.shape, a.dtype) for a in arrays],
        input_output_aliases={i: i for i in range(len(arrays))},
        cost_estimate=BRIEF,
    )(*arrays)


def ring(count, shift):
    return [(i, (i + shift) % count) for i in range(count)]


def swap_cores(a):
    return lax.ppermute(a, "core", [(0, 1), (1, 0)])


def turn(a, shift):
    pairs = [(i * 4 + j, (j + shift) % 4 * 4 + i) for i in range(4) for j in range(4)]
    return lax.ppermute(a, ("x", "y"), pairs)


def sum_prefix(terms, core):
    shape = terms.shape[1:]
    keep = jnp.where(core == 0, terms[0], terms[1])
    send = jnp.where(core == 0, terms[1], terms[0])
    half = (keep + swap_cores(send)).reshape(-1, shape[-1])
    half = lax.all_to_all(half, ("x", "z"), 0, 0, tiled=True)
    share = jnp.sum(half.reshape(32, -1, shape[-1]), axis=0, keepdims=True)
    half = jnp.broadcast_to(share, (32,) + share.shape[1:]).reshape(half.shape)
    half = lax.all_to_all(half, ("x", "z"), 0, 0, tiled=True).reshape(shape)
    other = swap_cores(half)
    return jnp.where(core == 0, half, other), jnp.where(core == 0, other, half)


def shards(queries, keys, values, prefix_keys, prefix_values, dout, key_weight, value_weight):
    y = lax.axis_index("y").astype(jnp.int32).reshape(1)
    core = lax.axis_index("core")

    unit = jnp.concatenate(
        [w[:, :, h : h + HD] for h in (0, HD) for w in (key_weight, value_weight)], axis=2
    )
    weights = lax.all_gather(turn(unit, 0), ("x", "z", "core"), axis=0)
    weights = weights.reshape((4, 8, 2) + unit.shape)

    grad_queries, flat, terms = attend_back(
        queries, keys, values, prefix_keys, prefix_values, dout
    )
    flats = [flat] + [lax.ppermute(flat, "y", ring(4, q)) for q in (1, 2, 3)]
    grad_prefix_keys, grad_prefix_values = sum_prefix(terms, core)
    *flats, grad_prefix_keys, grad_prefix_values = gate(
        *flats, grad_prefix_keys, grad_prefix_values
    )
    grad_input = project(flats, weights, y)
    return grad_queries, grad_input, grad_prefix_keys, grad_prefix_values


def solution(mesh):
    mesh = Mesh(mesh.devices.reshape(4, 8, 2, 4), ("x", "z", "core", "y"))
    dp = ("x", "z", "core")
    split = P(None, dp, "y")
    shared = P(None, None, "y")
    in_specs = (split, split, split, shared, shared, split, split, split)
    out_specs = (split, split, shared, shared)
    return jax.shard_map(shards, mesh=mesh, in_specs=in_specs, out_specs=out_specs, check_vma=False)
```

time: 175 us -> 152 us (0.87)
  blocking collectives: 16.4 us -> 37.7 us
  starting transfers between devices: 38 us -> 18.1 us
  waiting for transfers between devices: 60.9 us -> 45.1 us
  local copies, waits for them, and re-layouts: 9.43 us -> 3.19 us
  Pallas kernels: 32.4 us -> 30.5 us
    all_to_all x1, blocking collectives: 16.4 us -> 37.7 us  [sum_prefix(): half = lax.all_to_all(half, ('x', 'z'), 0, 0, tiled=True)]
    ppermute x4, starting transfers between devices: 22.7 us -> 4.36 us  [the longest x3 3.68 us: shards(): flats = [flat] + [lax.ppermute(flat, 'y', ring(4, q)) for q in (1, 2, 3)]]
    ppermute x4, waiting for transfers between devices: 22.3 us -> 8.95 us  [the longest x3 8.95 us: shards(): flats = [flat] + [lax.ppermute(flat, 'y', ring(4, q)) for q in (1, 2, 3)]]
    all_gather x1, waiting for transfers between devices: 37.4 us -> 26.2 us  [shards(): weights = lax.all_gather(turn(unit, 0), ('x', 'z', 'core'), axis=0)]
    unnamed x18 -> x10, local copies, waits for them, and re-layouts: 9.41 us -> 1.51 us
    all_to_all x1, waiting for transfers between devices: 0.01 us -> 7.57 us  [sum_prefix(): half = lax.all_to_all(half, ('x', 'z'), 0, 0, tiled=True).reshape(shape)]
    pallas_call x1, Pallas kernels: 2.18 us -> 0.01 us  [gate(): pl.pallas_call(gate_kernel, in_specs=anywhere, out_specs=anywhere, out_sh...]
    all_to_all x1, starting transfers between devices: 8.57 us -> 6.64 us  [sum_prefix(): half = lax.all_to_all(half, ('x', 'z'), 0, 0, tiled=True).reshape(shape)]
  transfers between devices with their start and end apart: 13 -> 8, of which waited for: 4 -> 6; matrix products, arithmetic and copies ran while one was open for 1% -> 3% of each run, Pallas kernels for 17% -> 12%
where the time goes in v2:
time: 152 us
  waiting for transfers between devices  45.1 us (30%)
  blocking collectives  37.7 us (25%)
  Pallas kernels  30.5 us (20%)
  starting transfers between devices  18.1 us (12%)
  between operations  14.1 us (9%)
  local copies, waits for them, and re-layouts  3.19 us (2%)
  other arithmetic  3.11 us (2%)
    all_to_all x1, blocking collectives, sum_prefix(): half = lax.all_to_all(half, ('x', 'z'), 0, 0, tiled=True)  37.7 us
    all_gather x1, waiting for transfers between devices, shards(): weights = lax.all_gather(turn(unit, 0), ('x', 'z', 'core'), axis=0)  26.2 us
    pallas_call x1, Pallas kernels, attend_back(): pl.pallas_call(attend_kernel, grid=(layers, heads), in_specs=[wide, own,...  18.7 us
    pallas_call x1, Pallas kernels, project(): pl.pallas_call(project_kernel, grid_spec=pltpu.PrefetchScalarGridSpec(num...  11.8 us
    ppermute x3, waiting for transfers between devices, shards(): flats = [flat] + [lax.ppermute(flat, 'y', ring(4, q)) for q in (1, 2, 3)]  8.95 us
    all_to_all x1, waiting for transfers between devices, sum_prefix(): half = lax.all_to_all(half, ('x', 'z'), 0, 0, tiled=True).reshape(shape)  7.57 us
    ppermute x2, starting transfers between devices, swap_cores(): return lax.ppermute(a, 'core', [(0, 1), (1, 0)])  7.07 us
    all_to_all x1, starting transfers between devices, sum_prefix(): half = lax.all_to_all(half, ('x', 'z'), 0, 0, tiled=True).reshape(shape)  6.64 us
  transfers between devices with their start and end apart: 8, of which 6 were waited for; matrix products, arithmetic and copies ran while one was open for 3% of the time, Pallas kernels for 12%

profile of v2, /device:TPU:1, one launch (start us, length us, event | category | flops | bytes accessed | tf_op | source)
XLA Modules:
  0.0 151.7 jit_solution(4072393068431320423)
XLA Ops:
  7.2 0.0 all-gather.3.cloned.1.call-start
  7.2 1.0 fusion
  8.2 0.7 collective-permute-start.5
  8.9 0.0 collective-permute-done.5
  8.9 0.0 copy-start.4
  8.9 0.7 copy-done.4
  9.6 0.0 all-gather.3.cloned.1.call-update
  9.6 18.7 %shard_map.111 = (bf16[2,256,2048]{2,1,0:T(8,128)(2,1)}, bf16[2,256,512]{2,1,0:T(8,128)(2,1)}, f32[2,2,128,256]{3,2,1,0:T(8,128)}) custom-call(bf16[2,256,2048]{2,1,0:T(8,128)(2,1)} %q_ref.1, bf16[2,256,256]{2,1,0:T(8,128)(2,1)} %k_ref.1, bf16[2,256,256]{2,1,0:T(8,128)(2,1)} %v_ref.1, bf16[2,128,256]{2,1,0:T(8,128)(2,1)} %pk_ref.1, ...), custom_call_target="tpu_custom_call" | custom-call | flops 2000000000 | bytes 16000000 | tf_op jit(solution)/shard_map/pallas_call | solution.py:80
  28.3 0.0 copy-start
  28.3 1.1 select_bitcast_fusion
  29.4 3.3 %collective-permute-start.3 = (f32[2,128,256]{2,1,0:T(8,128)S(1)}, f32[2,128,256]{2,1,0:T(8,128)S(1)}, u32[]{:S(2)}, u32[]{:S(2)}) collective-permute-start(f32[2,128,256]{2,1,0:T(8,128)S(1)} %select_bitcast_fusion), channel_id=1, source_target_pairs={{0,4},{4,0},{1,5},{5,1},{2,6},{6,2},{3,7},{7,3},{8,12},{12,8},{9,1... | collective-permute-start | bytes 786440 | tf_op jit(solution)/shard_map/ppermute | solution.py:150
  32.8 1.2 collective-permute-done.3
  33.9 1.1 bitcast_add_fusion
  35.0 37.7 %all_to_all.15 = f32[32,8,256]{2,1,0:T(8,128)S(1)} all-to-all(f32[32,8,256]{2,1,0:T(8,128)S(1)} %bitcast.17), channel_id=1, replica_groups=mesh['x'=4,'z'=8,'core'=2,'y'=4] {'x','z'}, dimensions={0} | all-to-all | bytes 524288 | tf_op jit(solution)/shard_map/all_to_all | solution.py:163
  72.7 0.7 broadcast_in_dim.2
  73.5 6.6 %all-to-all-start.1 = ((f32[32,8,256]{2,1,0:T(8,128)}), f32[32,8,256]{2,1,0:T(8,128)S(1)}, u32[]{:S(2)}, u32[]{:S(2)}) async-start(f32[32,8,256]{2,1,0:T(8,128)} %broadcast_in_dim.2), calls=%async_computation.1 | async-start | bytes 524288 | tf_op jit(solution)/shard_map/all_to_all | solution.py:166
  80.1 0.0 copy-done
  80.1 0.7 collective-permute-start
  80.8 1.8 %collective-permute-start.1 = (bf16[2,256,512]{2,1,0:T(8,128)(2,1)S(1)}, bf16[2,256,512]{2,1,0:T(8,128)(2,1)S(1)}, u32[]{:S(2)}, u32[]{:S(2)}) collective-permute-start(bf16[2,256,512]{2,1,0:T(8,128)(2,1)S(1)} %copy-done), channel_id=1, source_target_pairs={{0,2},{1,3},{2,0},{3,1},{4,6},{5,7},{6,4},{7,5},{8,10},{9,11},{10,... | collective-permute-start | bytes 1572872 | tf_op jit(solution)/shard_map/ppermute | solution.py:184
  82.6 1.1 collective-permute-start.2
  83.8 7.6 %all-to-all-done.1 = f32[32,8,256]{2,1,0:T(8,128)S(1)} async-done(((f32[32,8,256]{2,1,0:T(8,128)}), f32[32,8,256]{2,1,0:T(8,128)S(1)}, u32[]{:S(2)}, u32[]{:S(2)}) %all-to-all-start.1) | async-done | bytes 262176 | tf_op jit(solution)/shard_map/all_to_all | solution.py:166
  91.4 3.7 %collective-permute-start.4 = (f32[2,128,256]{2,1,0:T(8,128)S(1)}, f32[2,128,256]{2,1,0:T(8,128)S(1)}, u32[]{:S(2)}, u32[]{:S(2)}) collective-permute-start(f32[2,128,256]{2,1,0:T(8,128)S(1)} %bitcast.15), channel_id=1, source_target_pairs={{0,4},{4,0},{1,5},{5,1},{2,6},{6,2},{3,7},{7,3},{8,12},{12,8},{9,1... | collective-permute-start | bytes 786440 | tf_op jit(solution)/shard_map/ppermute | solution.py:150
  95.1 1.2 collective-permute-done.4
  96.2 0.8 broadcast_select_fusion
  97.1 0.0 collective-permute-done.refs_1_
  97.1 0.0 copy-start.1
  97.1 7.5 %collective-permute-done.1.refs_2_ = bf16[2,256,512]{2,1,0:T(8,128)(2,1)S(1)} collective-permute-done((bf16[2,256,512]{2,1,0:T(8,128)(2,1)S(1)}, bf16[2,256,512]{2,1,0:T(8,128)(2,1)S(1)}, u32[]{:S(2)}, u32[]{:S(2)}) %collective-permute-start.1) | collective-permute-done | bytes 524320 | tf_op jit(solution)/shard_map/ppermute | solution.py:184
  104.6 0.0 copy-start.2
  104.6 1.4 collective-permute-done.2.refs_3_
  106.0 0.0 copy-start.3
  106.0 0.0 copy-done.1
  106.0 0.0 copy-done.2
  106.1 0.8 copy-done.3
  106.9 26.2 %all-gather.3.cloned.1.call-done = bf16[128,128,512]{2,1,0:T(8,128)(2,1)} async-done(((bf16[2,128,512]{2,1,0:T(8,128)(2,1)}), bf16[128,128,512]{2,1,0:T(8,128)(2,1)}) %all-gather.3.cloned.1.call-update) | async-done | bytes 16777232 | tf_op jit(solution)/shard_map/all_gather | solution.py:178
  133.1 11.8 %shard_map.113 = bf16[2,256,2048]{2,1,0:T(8,128)(2,1)} custom-call(s32[1]{0:T(128)} %bitcast.y_ref, bf16[2,256,512]{2,1,0:T(8,128)(2,1)} %get-tuple-element.16.f0, bf16[2,256,512]{2,1,0:T(8,128)(2,1)} %get-tuple-element.17.f1, bf16[2,256,512]{2,1,0:T(8,128)(2,1)} %get-tuple-element.18.f2, bf16[2,256,512]{2,1,0:T(8,128)(2,1)} %get-tuple-element.19.f3, ...), custom_call_target="tpu_custom_call" | custom-call | flops 2000000000 | bytes 16000000 | tf_op jit(solution)/shard_map/pallas_call | solution.py:115
  (3 shorter events, 0.1 us)
Async XLA Ops:
  7.2 125.9 %all-gather.3.cloned.1.call-start = ((), (), s32[]{:S(2)}) async-start(), calls=%async_computation.2 | async-start | bytes 17039360 | tf_op jit(solution)/shard_map/all_gather | solution.py:178
  8.2 0.7 collective-permute-start.5
  8.9 0.7 copy-start.4
  28.3 51.8 %copy-start = (bf16[2,256,512]{2,1,0:T(8,128)(2,1)S(1)}, bf16[2,256,512]{2,1,0:T(8,128)(2,1)}, u32[]{:S(2)}) copy-start(bf16[2,256,512]{2,1,0:T(8,128)(2,1)} %get-tuple-element.14.refs_0_) | copy-start | bytes 1572868
  29.4 4.5 %collective-permute-start.3 = (f32[2,128,256]{2,1,0:T(8,128)S(1)}, f32[2,128,256]{2,1,0:T(8,128)S(1)}, u32[]{:S(2)}, u32[]{:S(2)}) collective-permute-start(f32[2,128,256]{2,1,0:T(8,128)S(1)} %select_bitcast_fusion), channel_id=1, source_target_pairs={{0,4},{4,0},{1,5},{5,1},{2,6},{6,2},{3,7},{7,3},{8,12},{12,8},{9,1... | collective-permute-start | bytes 786440 | tf_op jit(solution)/shard_map/ppermute | solution.py:150
  73.5 17.9 %all-to-all-start.1 = ((f32[32,8,256]{2,1,0:T(8,128)}), f32[32,8,256]{2,1,0:T(8,128)S(1)}, u32[]{:S(2)}, u32[]{:S(2)}) async-start(f32[32,8,256]{2,1,0:T(8,128)} %broadcast_in_dim.2), calls=%async_computation.1 | async-start | bytes 524288 | tf_op jit(solution)/shard_map/all_to_all | solution.py:166
  80.1 17.0 %collective-permute-start = (bf16[2,256,512]{2,1,0:T(8,128)(2,1)S(1)}, bf16[2,256,512]{2,1,0:T(8,128)(2,1)S(1)}, u32[]{:S(2)}, u32[]{:S(2)}) collective-permute-start(bf16[2,256,512]{2,1,0:T(8,128)(2,1)S(1)} %copy-done), channel_id=1, source_target_pairs={{0,1},{1,2},{2,3},{3,0},{4,5},{5,6},{6,7},{7,4},{8,9},{9,10},{10,1... | collective-permute-start | bytes 1572872 | tf_op jit(solution)/shard_map/ppermute | solution.py:184
  80.8 23.8 %collective-permute-start.1 = (bf16[2,256,512]{2,1,0:T(8,128)(2,1)S(1)}, bf16[2,256,512]{2,1,0:T(8,128)(2,1)S(1)}, u32[]{:S(2)}, u32[]{:S(2)}) collective-permute-start(bf16[2,256,512]{2,1,0:T(8,128)(2,1)S(1)} %copy-done), channel_id=1, source_target_pairs={{0,2},{1,3},{2,0},{3,1},{4,6},{5,7},{6,4},{7,5},{8,10},{9,11},{10,... | collective-permute-start | bytes 1572872 | tf_op jit(solution)/shard_map/ppermute | solution.py:184
  82.6 23.4 %collective-permute-start.2 = (bf16[2,256,512]{2,1,0:T(8,128)(2,1)S(1)}, bf16[2,256,512]{2,1,0:T(8,128)(2,1)S(1)}, u32[]{:S(2)}, u32[]{:S(2)}) collective-permute-start(bf16[2,256,512]{2,1,0:T(8,128)(2,1)S(1)} %copy-done), channel_id=1, source_target_pairs={{0,3},{1,0},{2,1},{3,2},{4,7},{5,4},{6,5},{7,6},{8,11},{9,8},{10,9... | collective-permute-start | bytes 1572872 | tf_op jit(solution)/shard_map/ppermute | solution.py:184
  91.4 4.9 %collective-permute-start.4 = (f32[2,128,256]{2,1,0:T(8,128)S(1)}, f32[2,128,256]{2,1,0:T(8,128)S(1)}, u32[]{:S(2)}, u32[]{:S(2)}) collective-permute-start(f32[2,128,256]{2,1,0:T(8,128)S(1)} %bitcast.15), channel_id=1, source_target_pairs={{0,4},{4,0},{1,5},{5,1},{2,6},{6,2},{3,7},{7,3},{8,12},{12,8},{9,1... | collective-permute-start | bytes 786440 | tf_op jit(solution)/shard_map/ppermute | solution.py:150
  97.1 9.0 %copy-start.1 = (bf16[2,256,512]{2,1,0:T(8,128)(2,1)}, bf16[2,256,512]{2,1,0:T(8,128)(2,1)S(1)}, u32[]{:S(2)}) copy-start(bf16[2,256,512]{2,1,0:T(8,128)(2,1)S(1)} %collective-permute-done.refs_1_) | copy-start | bytes 1572868
  104.6 1.4 copy-start.2
  106.0 0.8 copy-start.3
Sparse Core Ops, SparseCore 0:
  10.8 122.2 all-gather.2

commit v3 on v2

--- a/solution.py
+++ b/solution.py
@@ -66,7 +66,7 @@
         high = terms[1][split:] * scale
         flat_ref[0, :half, i * HD : (i + 1) * HD] = low[PREFIX:].astype(jnp.bfloat16)
         flat_ref[0, half:, i * HD : (i + 1) * HD] = high.astype(jnp.bfloat16)
-        terms_ref[i, 0] = low[:PREFIX]
+        terms_ref[i, 0, 0] = low[:PREFIX]
 
 
 def attend_back(queries, keys, values, prefix_keys, prefix_values, dout):
@@ -76,7 +76,7 @@
     own = pl.BlockSpec((1, LEN, HD), lambda l, h: (l, 0, h))
     pre = pl.BlockSpec((1, PREFIX, HD), lambda l, h: (l, 0, h))
     flat = pl.BlockSpec((1, LEN, 2 * HD), lambda l, h: (l, 0, h))
-    terms = pl.BlockSpec((2, 1, PREFIX, HD), lambda l, h: (0, l, 0, h))
+    terms = pl.BlockSpec((2, 1, 1, PREFIX, HD), lambda l, h: (0, l, h, 0, 0))
     return pl.pallas_call(
         attend_kernel,
         grid=(layers, heads),
@@ -85,7 +85,7 @@
         out_shape=[
             jax.ShapeDtypeStruct(queries.shape, jnp.bfloat16),
             jax.ShapeDtypeStruct((layers, LEN, 2 * width), jnp.bfloat16),
-            jax.ShapeDtypeStruct((2, layers, PREFIX, width), jnp.float32),
+            jax.ShapeDtypeStruct((2, layers, heads, PREFIX, HD), jnp.float32),
         ],
         compiler_params=pltpu.CompilerParams(vmem_limit_bytes=VMEM_LIMIT),
         cost_estimate=COST,
@@ -103,13 +103,13 @@
 def project(flats, weights, y):
     layers, tokens, depth = flats[0].shape
     rows = weights.shape[4]
-    step = 2
+    step = 4
     flat_spec = pl.BlockSpec((1, tokens, depth), lambda l, n, y_ref: (l, 0, 0))
 
     def weight_spec(shift):
         return pl.BlockSpec(
             (1, step, 2, 1, rows, depth),
-            lambda l, n, y_ref: (lax.rem(y_ref[0] + 4 - shift, 4), n, 0, l, 0, 0),
+            lambda l, n, y_ref: (lax.rem(y_ref[0] + 4 - shift + 2 * l, 4), n, 0, l, 0, 0),
         )
 
     return pl.pallas_call(
@@ -155,17 +155,24 @@
     return lax.ppermute(a, ("x", "y"), pairs)
 
 
+def exchange(a):
+    return lax.all_to_all(a, ("x", "z"), 0, 0, tiled=True)
+
+
 def sum_prefix(terms, core):
-    shape = terms.shape[1:]
     keep = jnp.where(core == 0, terms[0], terms[1])
     send = jnp.where(core == 0, terms[1], terms[0])
-    half = (keep + swap_cores(send)).reshape(-1, shape[-1])
-    half = lax.all_to_all(half, ("x", "z"), 0, 0, tiled=True)
-    share = jnp.sum(half.reshape(32, -1, shape[-1]), axis=0, keepdims=True)
-    half = jnp.broadcast_to(share, (32,) + share.shape[1:]).reshape(half.shape)
-    half = lax.all_to_all(half, ("x", "z"), 0, 0, tiled=True).reshape(shape)
-    other = swap_cores(half)
-    return jnp.where(core == 0, half, other), jnp.where(core == 0, other, half)
+    share = exchange((keep + swap_cores(send)).astype(jnp.bfloat16).reshape(-1, HD))
+    share = jnp.sum(share.reshape(32, -1, HD).astype(jnp.float32), axis=0, keepdims=True)
+    share = jnp.broadcast_to(share.astype(jnp.bfloat16), (32,) + share.shape[1:])
+    share = exchange(share.reshape(-1, HD))
+    other = swap_cores(share)
+
+    def whole(a, b):
+        a = jnp.where(core == 0, a, b).reshape(terms.shape[1:]).transpose(0, 2, 1, 3)
+        return a.astype(jnp.float32).reshape(2, PREFIX, -1)
+
+    return whole(share, other), whole(other, share)
 
 
 def shards(queries, keys, values, prefix_keys, prefix_values, dout, key_weight, value_weight):
@@ -175,7 +182,8 @@
     unit = jnp.concatenate(
         [w[:, :, h : h + HD] for h in (0, HD) for w in (key_weight, value_weight)], axis=2
     )
-    weights = lax.all_gather(turn(unit, 0), ("x", "z", "core"), axis=0)
+    turned = jnp.stack([turn(unit[0], 0), turn(unit[1], 2)])
+    weights = lax.all_gather(turned, ("x", "z", "core"), axis=0)
     weights = weights.reshape((4, 8, 2) + unit.shape)
 
     grad_queries, flat, terms = attend_back(

time: 152 us -> 145 us (0.954)
  starting transfers between devices: 18.1 us -> 13.4 us
  waiting for transfers between devices: 45.1 us -> 40.7 us
  blocking collectives: 37.7 us -> 41.8 us
  Pallas kernels: 30.5 us -> 28.9 us
    ppermute x3, waiting for transfers between devices: 8.95 us -> 22.9 us  [shards(): flats = [flat] + [lax.ppermute(flat, 'y', ring(4, q)) for q in (1, 2, 3)]]
    all_gather x1, waiting for transfers between devices: 26.2 us -> 14.8 us  [shards(): weights = lax.all_gather(turned, ('x', 'z', 'core'), axis=0)]
    all_to_all x1 -> x0, waiting for transfers between devices: 7.57 us -> none  [sum_prefix(): half = lax.all_to_all(half, ('x', 'z'), 0, 0, tiled=True).reshape(shape)]
    all_to_all x1 -> x0, starting transfers between devices: 6.64 us -> none  [sum_prefix(): half = lax.all_to_all(half, ('x', 'z'), 0, 0, tiled=True).reshape(shape)]
    all_to_all x1 -> x2, blocking collectives: 37.7 us -> 41.8 us  [exchange(): return lax.all_to_all(a, ('x', 'z'), 0, 0, tiled=True)]
    ppermute x1 -> x2, starting transfers between devices: 0.68 us -> 4.31 us  [turn(): return lax.ppermute(a, ('x', 'y'), pairs)]
    ppermute x1 -> x2, waiting for transfers between devices: 0.01 us -> 1.87 us  [turn(): return lax.ppermute(a, ('x', 'y'), pairs)]
    pallas_call x1, Pallas kernels: 11.8 us -> 10.2 us  [project(): pl.pallas_call(project_kernel, grid_spec=pltpu.PrefetchScalarGridSpec(num...]
  transfers between devices with their start and end apart: 8 -> 8, of which waited for: 6 -> 5; matrix products, arithmetic and copies ran while one was open for 3% -> 2% of each run, Pallas kernels for 12% -> 13%
where the time goes in v3:
time: 145 us
  blocking collectives  41.8 us (29%)
  waiting for transfers between devices  40.7 us (28%)
  Pallas kernels  28.9 us (20%)
  between operations  14.1 us (10%)
  starting transfers between devices  13.4 us (9%)
  other arithmetic  3.87 us (3%)
  local copies, waits for them, and re-layouts  1.88 us (1%)
    all_to_all x2, blocking collectives, exchange(): return lax.all_to_all(a, ('x', 'z'), 0, 0, tiled=True)  41.8 us
    ppermute x3, waiting for transfers between devices, shards(): flats = [flat] + [lax.ppermute(flat, 'y', ring(4, q)) for q in (1, 2, 3)]  22.9 us
    pallas_call x1, Pallas kernels, attend_back(): pl.pallas_call(attend_kernel, grid=(layers, heads), in_specs=[wide, own,...  18.7 us
    all_gather x1, waiting for transfers between devices, shards(): weights = lax.all_gather(turned, ('x', 'z', 'core'), axis=0)  14.8 us
    pallas_call x1, Pallas kernels, project(): pl.pallas_call(project_kernel, grid_spec=pltpu.PrefetchScalarGridSpec(num...  10.2 us
    ppermute x2, starting transfers between devices, swap_cores(): return lax.ppermute(a, 'core', [(0, 1), (1, 0)])  6.39 us
    ppermute x2, starting transfers between devices, turn(): return lax.ppermute(a, ('x', 'y'), pairs)  4.31 us
  transfers between devices with their start and end apart: 8, of which 5 were waited for; matrix products, arithmetic and copies ran while one was open for 2% of the time, Pallas kernels for 13%

profile of v3, /device:TPU:1, one launch (start us, length us, event | category | flops | bytes accessed | tf_op | source)
XLA Modules:
  0.0 144.6 jit_solution(4069210218064717582)
XLA Ops:
  7.2 0.0 all-gather.3.cloned.1.call-start
  7.2 1.0 fusion.1
  8.2 3.7 %collective-permute-start.6 = (bf16[128,512]{1,0:T(8,128)(2,1)S(1)}, bf16[128,512]{1,0:T(8,128)(2,1)S(1)}, u32[]{:S(2)}, u32[]{:S(2)}) collective-permute-start(bf16[128,512]{1,0:T(8,128)(2,1)S(1)} %get-tuple-element.23), channel_id=1, source_target_pairs={{0,128},{1,192},{2,0},{3,64},{64,129},{65,193},{66,1},{67,65},{128... | collective-permute-start | bytes 393224 | tf_op jit(solution)/shard_map/ppermute | solution.py:155
  11.9 0.7 collective-permute-start.5
  12.6 1.9 %collective-permute-done.6 = bf16[128,512]{1,0:T(8,128)(2,1)S(1)} collective-permute-done((bf16[128,512]{1,0:T(8,128)(2,1)S(1)}, bf16[128,512]{1,0:T(8,128)(2,1)S(1)}, u32[]{:S(2)}, u32[]{:S(2)}) %collective-permute-start.6) | collective-permute-done | bytes 131104 | tf_op jit(solution)/shard_map/ppermute | solution.py:155
  14.4 0.0 collective-permute-done.5
  14.4 0.7 pad_maximum_fusion.1
  15.2 0.0 all-gather.3.cloned.1.call-update
  15.2 18.7 %shard_map.111 = (bf16[2,256,2048]{2,1,0:T(8,128)(2,1)}, bf16[2,256,512]{2,1,0:T(8,128)(2,1)}, f32[2,2,2,128,128]{4,3,2,1,0:T(8,128)}) custom-call(bf16[2,256,2048]{2,1,0:T(8,128)(2,1)} %q_ref.1, bf16[2,256,256]{2,1,0:T(8,128)(2,1)} %k_ref.1, bf16[2,256,256]{2,1,0:T(8,128)(2,1)} %v_ref.1, bf16[2,128,256]{2,1,0:T(8,128)(2,1)} %pk_ref.1, ...), custom_call_target="tpu_custom_call" | custom-call | flops 2000000000 | bytes 16000000 | tf_op jit(solution)/shard_map/pallas_call | solution.py:80
  33.9 0.0 copy-start
  33.9 1.1 select_bitcast_fusion
  35.0 3.8 %collective-permute-start.3 = (f32[2,2,128,128]{3,2,1,0:T(8,128)S(1)}, f32[2,2,128,128]{3,2,1,0:T(8,128)S(1)}, u32[]{:S(2)}, u32[]{:S(2)}) collective-permute-start(f32[2,2,128,128]{3,2,1,0:T(8,128)S(1)} %select_bitcast_fusion), channel_id=1, source_target_pairs={{0,4},{4,0},{1,5},{5,1},{2,6},{6,2},{3,7},{7,3},{8,12},{12,8},{9,1... | collective-permute-start | bytes 786440 | tf_op jit(solution)/shard_map/ppermute | solution.py:150
  38.8 1.2 collective-permute-done.3
  39.9 1.1 fusion
  41.0 27.7 %all_to_all.18 = bf16[32,16,128]{2,1,0:T(8,128)(2,1)S(1)} all-to-all(bf16[32,16,128]{2,1,0:T(8,128)(2,1)S(1)} %bitcast.39), channel_id=1, replica_groups=mesh['x'=4,'z'=8,'core'=2,'y'=4] {'x','z'}, dimensions={0} | all-to-all | bytes 262144 | tf_op jit(solution)/shard_map/all_to_all | solution.py:159
  68.8 14.1 %all_to_all.19 = bf16[32,16,128]{2,1,0:T(8,128)(2,1)S(1)} all-to-all(bf16[32,16,128]{2,1,0:T(8,128)(2,1)S(1)} %broadcast_in_dim.2), channel_id=1, replica_groups=mesh['x'=4,'z'=8,'core'=2,'y'=4] {'x','z'}, dimensions={0} | all-to-all | bytes 262144 | tf_op jit(solution)/shard_map/all_to_all | solution.py:159
  82.9 2.6 %collective-permute-start.4 = (bf16[512,128]{1,0:T(8,128)(2,1)S(1)}, bf16[512,128]{1,0:T(8,128)(2,1)S(1)}, u32[]{:S(2)}, u32[]{:S(2)}) collective-permute-start(bf16[512,128]{1,0:T(8,128)(2,1)S(1)} %bitcast.38), channel_id=1, source_target_pairs={{0,4},{4,0},{1,5},{5,1},{2,6},{6,2},{3,7},{7,3},{8,12},{12,8},{9,1... | collective-permute-start | bytes 393224 | tf_op jit(solution)/shard_map/ppermute | solution.py:150
  85.5 0.0 copy-done
  85.5 0.0 collective-permute-start
  85.5 0.1 collective-permute-start.1
  85.5 2.6 %collective-permute-start.2 = (bf16[2,256,512]{2,1,0:T(8,128)(2,1)S(1)}, bf16[2,256,512]{2,1,0:T(8,128)(2,1)S(1)}, u32[]{:S(2)}, u32[]{:S(2)}) collective-permute-start(bf16[2,256,512]{2,1,0:T(8,128)(2,1)S(1)} %copy-done), channel_id=1, source_target_pairs={{0,3},{1,0},{2,1},{3,2},{4,7},{5,4},{6,5},{7,6},{8,11},{9,8},{10,9... | collective-permute-start | bytes 1572872 | tf_op jit(solution)/shard_map/ppermute | solution.py:192
  88.2 0.0 collective-permute-done.4
  88.2 0.8 copy_bitcast_fusion
  89.0 22.6 %collective-permute-done.refs_1_ = bf16[2,256,512]{2,1,0:T(8,128)(2,1)S(1)} collective-permute-done((bf16[2,256,512]{2,1,0:T(8,128)(2,1)S(1)}, bf16[2,256,512]{2,1,0:T(8,128)(2,1)S(1)}, u32[]{:S(2)}, u32[]{:S(2)}) %collective-permute-start) | collective-permute-done | bytes 524320 | tf_op jit(solution)/shard_map/ppermute | solution.py:192
  111.6 0.0 copy-start.1
  111.6 0.0 collective-permute-done.1.refs_2_
  111.6 0.0 copy-start.2
  111.6 0.3 collective-permute-done.2.refs_3_
  111.9 0.0 copy-start.3
  111.9 0.5 copy-done.1
  112.4 0.2 copy-done.2
  112.6 0.2 copy-done.3
  112.8 14.8 %all-gather.3.cloned.1.call-done = bf16[128,128,512]{2,1,0:T(8,128)(2,1)} async-done(((bf16[2,128,512]{2,1,0:T(8,128)(2,1)}), bf16[128,128,512]{2,1,0:T(8,128)(2,1)}) %all-gather.3.cloned.1.call-update) | async-done | bytes 16777232 | tf_op jit(solution)/shard_map/all_gather | solution.py:186
  127.5 10.2 %shard_map.113 = bf16[2,256,2048]{2,1,0:T(8,128)(2,1)} custom-call(s32[1]{0:T(128)} %bitcast.y_ref, bf16[2,256,512]{2,1,0:T(8,128)(2,1)} %get-tuple-element.16.f0, bf16[2,256,512]{2,1,0:T(8,128)(2,1)} %get-tuple-element.17.f1, bf16[2,256,512]{2,1,0:T(8,128)(2,1)} %get-tuple-element.18.f2, bf16[2,256,512]{2,1,0:T(8,128)(2,1)} %get-tuple-element.19.f3, ...), custom_call_target="tpu_custom_call" | custom-call | flops 2000000000 | bytes 16000000 | tf_op jit(solution)/shard_map/pallas_call | solution.py:115
  (6 shorter events, 0.1 us)
Async XLA Ops:
  7.2 120.4 %all-gather.3.cloned.1.call-start = ((), (), s32[]{:S(2)}) async-start(), calls=%async_computation.2 | async-start | bytes 17039360 | tf_op jit(solution)/shard_map/all_gather | solution.py:186
  8.2 6.2 %collective-permute-start.6 = (bf16[128,512]{1,0:T(8,128)(2,1)S(1)}, bf16[128,512]{1,0:T(8,128)(2,1)S(1)}, u32[]{:S(2)}, u32[]{:S(2)}) collective-permute-start(bf16[128,512]{1,0:T(8,128)(2,1)S(1)} %get-tuple-element.23), channel_id=1, source_target_pairs={{0,128},{1,192},{2,0},{3,64},{64,129},{65,193},{66,1},{67,65},{128... | collective-permute-start | bytes 393224 | tf_op jit(solution)/shard_map/ppermute | solution.py:155
  11.9 2.5 %collective-permute-start.5 = (bf16[128,512]{1,0:T(8,128)(2,1)S(1)}, bf16[128,512]{1,0:T(8,128)(2,1)S(1)}, u32[]{:S(2)}, u32[]{:S(2)}) collective-permute-start(bf16[128,512]{1,0:T(8,128)(2,1)S(1)} %get-tuple-element.22), channel_id=1, source_target_pairs={{0,0},{1,64},{2,128},{3,192},{64,1},{65,65},{66,129},{67,193},{128... | collective-permute-start | bytes 393224 | tf_op jit(solution)/shard_map/ppermute | solution.py:155
  33.9 51.6 %copy-start = (bf16[2,256,512]{2,1,0:T(8,128)(2,1)S(1)}, bf16[2,256,512]{2,1,0:T(8,128)(2,1)}, u32[]{:S(2)}) copy-start(bf16[2,256,512]{2,1,0:T(8,128)(2,1)} %get-tuple-element.14.refs_0_) | copy-start | bytes 1572868
  35.0 4.9 %collective-permute-start.3 = (f32[2,2,128,128]{3,2,1,0:T(8,128)S(1)}, f32[2,2,128,128]{3,2,1,0:T(8,128)S(1)}, u32[]{:S(2)}, u32[]{:S(2)}) collective-permute-start(f32[2,2,128,128]{3,2,1,0:T(8,128)S(1)} %select_bitcast_fusion), channel_id=1, source_target_pairs={{0,4},{4,0},{1,5},{5,1},{2,6},{6,2},{3,7},{7,3},{8,12},{12,8},{9,1... | collective-permute-start | bytes 786440 | tf_op jit(solution)/shard_map/ppermute | solution.py:150
  82.9 5.3 %collective-permute-start.4 = (bf16[512,128]{1,0:T(8,128)(2,1)S(1)}, bf16[512,128]{1,0:T(8,128)(2,1)S(1)}, u32[]{:S(2)}, u32[]{:S(2)}) collective-permute-start(bf16[512,128]{1,0:T(8,128)(2,1)S(1)} %bitcast.38), channel_id=1, source_target_pairs={{0,4},{4,0},{1,5},{5,1},{2,6},{6,2},{3,7},{7,3},{8,12},{12,8},{9,1... | collective-permute-start | bytes 393224 | tf_op jit(solution)/shard_map/ppermute | solution.py:150
  85.5 26.1 %collective-permute-start = (bf16[2,256,512]{2,1,0:T(8,128)(2,1)S(1)}, bf16[2,256,512]{2,1,0:T(8,128)(2,1)S(1)}, u32[]{:S(2)}, u32[]{:S(2)}) collective-permute-start(bf16[2,256,512]{2,1,0:T(8,128)(2,1)S(1)} %copy-done), channel_id=1, source_target_pairs={{0,1},{1,2},{2,3},{3,0},{4,5},{5,6},{6,7},{7,4},{8,9},{9,10},{10,1... | collective-permute-start | bytes 1572872 | tf_op jit(solution)/shard_map/ppermute | solution.py:192
  85.5 26.1 %collective-permute-start.1 = (bf16[2,256,512]{2,1,0:T(8,128)(2,1)S(1)}, bf16[2,256,512]{2,1,0:T(8,128)(2,1)S(1)}, u32[]{:S(2)}, u32[]{:S(2)}) collective-permute-start(bf16[2,256,512]{2,1,0:T(8,128)(2,1)S(1)} %copy-done), channel_id=1, source_target_pairs={{0,2},{1,3},{2,0},{3,1},{4,6},{5,7},{6,4},{7,5},{8,10},{9,11},{10,... | collective-permute-start | bytes 1572872 | tf_op jit(solution)/shard_map/ppermute | solution.py:192
  85.5 26.4 %collective-permute-start.2 = (bf16[2,256,512]{2,1,0:T(8,128)(2,1)S(1)}, bf16[2,256,512]{2,1,0:T(8,128)(2,1)S(1)}, u32[]{:S(2)}, u32[]{:S(2)}) collective-permute-start(bf16[2,256,512]{2,1,0:T(8,128)(2,1)S(1)} %copy-done), channel_id=1, source_target_pairs={{0,3},{1,0},{2,1},{3,2},{4,7},{5,4},{6,5},{7,6},{8,11},{9,8},{10,9... | collective-permute-start | bytes 1572872 | tf_op jit(solution)/shard_map/ppermute | solution.py:192
  111.6 0.8 copy-start.1
  111.6 1.0 copy-start.2
  111.9 0.9 copy-start.3
Sparse Core Ops, SparseCore 0:
  15.3 112.1 all-gather.2

commit v4 on v3

--- a/solution.py
+++ b/solution.py
@@ -64,8 +64,9 @@
     for i, (terms, scale) in enumerate(((key_terms, SCALE), (value_terms, 1.0))):
         low = (terms[0] + terms[1][:split]) * scale
         high = terms[1][split:] * scale
-        flat_ref[0, :half, i * HD : (i + 1) * HD] = low[PREFIX:].astype(jnp.bfloat16)
-        flat_ref[0, half:, i * HD : (i + 1) * HD] = high.astype(jnp.bfloat16)
+        columns = pl.ds(pl.multiple_of((2 * i + pl.program_id(1)) * HD, HD), HD)
+        flat_ref[0, :half, columns] = low[PREFIX:].astype(jnp.bfloat16)
+        flat_ref[0, half:, columns] = high.astype(jnp.bfloat16)
         terms_ref[i, 0, 0] = low[:PREFIX]
 
 
@@ -75,7 +76,7 @@
     wide = pl.BlockSpec((1, LEN, GROUP * HD), lambda l, h: (l, 0, h))
     own = pl.BlockSpec((1, LEN, HD), lambda l, h: (l, 0, h))
     pre = pl.BlockSpec((1, PREFIX, HD), lambda l, h: (l, 0, h))
-    flat = pl.BlockSpec((1, LEN, 2 * HD), lambda l, h: (l, 0, h))
+    flat = pl.BlockSpec((1, LEN, 2 * width), lambda l, h: (l, 0, 0))
     terms = pl.BlockSpec((2, 1, 1, PREFIX, HD), lambda l, h: (0, l, h, 0, 0))
     return pl.pallas_call(
         attend_kernel,
@@ -92,10 +93,13 @@
     )(queries, keys, values, prefix_keys, prefix_values, dout)
 
 
-def project_kernel(y_ref, f0, f1, f2, f3, w0, w1, w2, w3, out_ref):
+def project_kernel(y_ref, f0, f1, f2, f3, *refs):
+    flats, weight_refs, out_ref = (f0, f1, f2, f3), refs[:-1], refs[-1]
     total = None
-    for f, w in zip((f0, f1, f2, f3), (w0, w1, w2, w3)):
-        term = dot(f[0], w[...].reshape(-1, w.shape[-1]), NT)
+    for s in range(4):
+        even, odd = weight_refs[2 * s], weight_refs[2 * s + 1]
+        rows = [w[0, n, 0, 0] for n in range(even.shape[1]) for w in (even, odd)]
+        term = dot(flats[s][0], jnp.concatenate(rows, axis=0), NT)
         total = term if total is None else total + term
     out_ref[0] = total.astype(jnp.bfloat16)
 
@@ -106,10 +110,10 @@
     step = 4
     flat_spec = pl.BlockSpec((1, tokens, depth), lambda l, n, y_ref: (l, 0, 0))
 
-    def weight_spec(shift):
+    def weight_spec(s, core):
         return pl.BlockSpec(
-            (1, step, 2, 1, rows, depth),
-            lambda l, n, y_ref: (lax.rem(y_ref[0] + 4 - shift + 2 * l, 4), n, 0, l, 0, 0),
+            (1, step, 1, 1, rows, depth),
+            lambda l, n, y_ref: (lax.rem(y_ref[0] + 4 - s + 2 * core, 4), n, core, l, 0, 0),
         )
 
     return pl.pallas_call(
@@ -117,13 +121,13 @@
         grid_spec=pltpu.PrefetchScalarGridSpec(
             num_scalar_prefetch=1,
             grid=(layers, 8 // step),
-            in_specs=[flat_spec] * 4 + [weight_spec(s) for s in range(4)],
+            in_specs=[flat_spec] * 4 + [weight_spec(s, core) for s in range(4) for core in range(2)],
             out_specs=pl.BlockSpec((1, tokens, step * 2 * rows), lambda l, n, y_ref: (l, 0, n)),
         ),
         out_shape=jax.ShapeDtypeStruct((layers, tokens, 16 * rows), jnp.bfloat16),
         compiler_params=pltpu.CompilerParams(vmem_limit_bytes=VMEM_LIMIT),
         cost_estimate=COST,
-    )(y, *flats, weights, weights, weights, weights)
+    )(y, *flats, *[weights] * 8)
 
 
 def gate_kernel(*refs):
@@ -151,8 +155,13 @@
 
 
 def turn(a, shift):
-    pairs = [(i * 4 + j, (j + shift) % 4 * 4 + i) for i in range(4) for j in range(4)]
-    return lax.ppermute(a, ("x", "y"), pairs)
+    pairs = []
+    for x in range(4):
+        for core in range(2):
+            for y in range(4):
+                there = ((y + 2 * core + shift) % 4 * 2 + core) * 4 + x
+                pairs.append(((x * 2 + core) * 4 + y, there))
+    return lax.ppermute(a, ("x", "core", "y"), pairs)
 
 
 def exchange(a):
@@ -179,12 +188,9 @@
     y = lax.axis_index("y").astype(jnp.int32).reshape(1)
     core = lax.axis_index("core")
 
-    unit = jnp.concatenate(
-        [w[:, :, h : h + HD] for h in (0, HD) for w in (key_weight, value_weight)], axis=2
-    )
-    turned = jnp.stack([turn(unit[0], 0), turn(unit[1], 2)])
+    turned = turn(jnp.concatenate([key_weight, value_weight], axis=2), 0)
     weights = lax.all_gather(turned, ("x", "z", "core"), axis=0)
-    weights = weights.reshape((4, 8, 2) + unit.shape)
+    weights = weights.reshape((4, 8, 2) + turned.shape)
 
     grad_queries, flat, terms = attend_back(
         queries, keys, values, prefix_keys, prefix_values, dout

time: 145 us -> 143 us (0.986)
  waiting for transfers between devices: 40.7 us -> 43.2 us
  starting transfers between devices: 13.4 us -> 11.1 us
  blocking collectives: 41.8 us -> 40.2 us
    ppermute x2, starting transfers between devices: 6.39 us -> 2.86 us  [swap_cores(): return lax.ppermute(a, 'core', [(0, 1), (1, 0)])]
    ppermute x2 -> x1, waiting for transfers between devices: 1.87 us -> 3.92 us  [turn(): return lax.ppermute(a, ('x', 'core', 'y'), pairs)]
    all_to_all x2, blocking collectives: 41.8 us -> 40.2 us  [exchange(): return lax.all_to_all(a, ('x', 'z'), 0, 0, tiled=True)]
    ppermute x2 -> x1, starting transfers between devices: 4.31 us -> 5.48 us  [turn(): return lax.ppermute(a, ('x', 'core', 'y'), pairs)]
  transfers between devices with their start and end apart: 8 -> 7, of which waited for: 5 -> 5; matrix products, arithmetic and copies ran while one was open for 2% -> 2% of each run, Pallas kernels for 13% -> 13%
where the time goes in v4:
time: 143 us
  waiting for transfers between devices  43.2 us (30%)
  blocking collectives  40.2 us (28%)
  Pallas kernels  29 us (20%)
  between operations  14.1 us (10%)
  starting transfers between devices  11.1 us (8%)
  other arithmetic  4.1 us (3%)
  local copies, waits for them, and re-layouts  1.6 us (1%)
    all_to_all x2, blocking collectives, exchange(): return lax.all_to_all(a, ('x', 'z'), 0, 0, tiled=True)  40.2 us
    ppermute x3, waiting for transfers between devices, shards(): flats = [flat] + [lax.ppermute(flat, 'y', ring(4, q)) for q in (1, 2, 3)]  22.9 us
    pallas_call x1, Pallas kernels, attend_back(): pl.pallas_call(attend_kernel, grid=(layers, heads), in_specs=[wide, own,...  18.8 us
    all_gather x1, waiting for transfers between devices, shards(): weights = lax.all_gather(turned, ('x', 'z', 'core'), axis=0)  14.9 us
    pallas_call x1, Pallas kernels, project(): pl.pallas_call(project_kernel, grid_spec=pltpu.PrefetchScalarGridSpec(num...  10.2 us
    ppermute x1, starting transfers between devices, turn(): return lax.ppermute(a, ('x', 'core', 'y'), pairs)  5.48 us
    ppermute x1, waiting for transfers between devices, turn(): return lax.ppermute(a, ('x', 'core', 'y'), pairs)  3.92 us
    ppermute x2, starting transfers between devices, swap_cores(): return lax.ppermute(a, 'core', [(0, 1), (1, 0)])  2.86 us
  transfers between devices with their start and end apart: 7, of which 5 were waited for; matrix products, arithmetic and copies ran while one was open for 2% of the time, Pallas kernels for 13%

profile of v4, /device:TPU:1, one launch (start us, length us, event | category | flops | bytes accessed | tf_op | source)
XLA Modules:
  0.0 143.2 jit_solution(4665449246243272120)
XLA Ops:
  7.2 0.0 all-gather.3.cloned.1.call-start
  7.2 1.0 pad_maximum_fusion
  8.2 5.5 %collective-permute-start.5 = (bf16[2,128,512]{2,1,0:T(8,128)(2,1)S(1)}, bf16[2,128,512]{2,1,0:T(8,128)(2,1)S(1)}, u32[]{:S(2)}, u32[]{:S(2)}) collective-permute-start(bf16[2,128,512]{2,1,0:T(8,128)(2,1)S(1)} %pad_maximum_fusion), channel_id=1, source_target_pairs={{0,0},{1,64},{2,128},{3,192},{4,132},{5,196},{6,4},{7,68},{64,1},{... | collective-permute-start | bytes 786440 | tf_op jit(solution)/shard_map/ppermute | solution.py:164
  13.7 3.9 %collective-permute-done.5 = bf16[2,128,512]{2,1,0:T(8,128)(2,1)S(1)} collective-permute-done((bf16[2,128,512]{2,1,0:T(8,128)(2,1)S(1)}, bf16[2,128,512]{2,1,0:T(8,128)(2,1)S(1)}, u32[]{:S(2)}, u32[]{:S(2)}) %collective-permute-start.5) | collective-permute-done | bytes 262176 | tf_op jit(solution)/shard_map/ppermute | solution.py:164
  17.6 0.0 copy-start.4
  17.6 0.7 copy-done.4
  18.3 0.0 all-gather.3.cloned.1.call-update
  18.3 18.8 %shard_map.111 = (bf16[2,256,2048]{2,1,0:T(8,128)(2,1)}, bf16[2,256,512]{2,1,0:T(8,128)(2,1)}, f32[2,2,2,128,128]{4,3,2,1,0:T(8,128)}) custom-call(bf16[2,256,2048]{2,1,0:T(8,128)(2,1)} %q_ref.1, bf16[2,256,256]{2,1,0:T(8,128)(2,1)} %k_ref.1, bf16[2,256,256]{2,1,0:T(8,128)(2,1)} %v_ref.1, bf16[2,128,256]{2,1,0:T(8,128)(2,1)} %pk_ref.1, ...), custom_call_target="tpu_custom_call" | custom-call | flops 2000000000 | bytes 16000000 | tf_op jit(solution)/shard_map/pallas_call | solution.py:81
  37.1 0.0 copy-start
  37.1 1.1 select_bitcast_fusion
  38.2 0.1 collective-permute-start.3
  38.3 1.5 %collective-permute-done.3 = f32[2,2,128,128]{3,2,1,0:T(8,128)S(1)} collective-permute-done((f32[2,2,128,128]{3,2,1,0:T(8,128)S(1)}, f32[2,2,128,128]{3,2,1,0:T(8,128)S(1)}, u32[]{:S(2)}, u32[]{:S(2)}) %collective-permute-start.3) | collective-permute-done | bytes 262176 | tf_op jit(solution)/shard_map/ppermute | solution.py:154
  39.9 1.1 fusion
  40.9 26.2 %all_to_all.18 = bf16[32,16,128]{2,1,0:T(8,128)(2,1)S(1)} all-to-all(bf16[32,16,128]{2,1,0:T(8,128)(2,1)S(1)} %bitcast.37), channel_id=1, replica_groups=mesh['x'=4,'z'=8,'core'=2,'y'=4] {'x','z'}, dimensions={0} | all-to-all | bytes 262144 | tf_op jit(solution)/shard_map/all_to_all | solution.py:168
  67.2 14.0 %all_to_all.19 = bf16[32,16,128]{2,1,0:T(8,128)(2,1)S(1)} all-to-all(bf16[32,16,128]{2,1,0:T(8,128)(2,1)S(1)} %broadcast_in_dim.2), channel_id=1, replica_groups=mesh['x'=4,'z'=8,'core'=2,'y'=4] {'x','z'}, dimensions={0} | all-to-all | bytes 262144 | tf_op jit(solution)/shard_map/all_to_all | solution.py:168
  81.2 2.8 %collective-permute-start.4 = (bf16[512,128]{1,0:T(8,128)(2,1)S(1)}, bf16[512,128]{1,0:T(8,128)(2,1)S(1)}, u32[]{:S(2)}, u32[]{:S(2)}) collective-permute-start(bf16[512,128]{1,0:T(8,128)(2,1)S(1)} %bitcast.36), channel_id=1, source_target_pairs={{0,4},{4,0},{1,5},{5,1},{2,6},{6,2},{3,7},{7,3},{8,12},{12,8},{9,1... | collective-permute-start | bytes 393224 | tf_op jit(solution)/shard_map/ppermute | solution.py:154
  83.9 0.0 copy-done
  83.9 0.0 collective-permute-start
  83.9 1.6 %collective-permute-start.1 = (bf16[2,256,512]{2,1,0:T(8,128)(2,1)S(1)}, bf16[2,256,512]{2,1,0:T(8,128)(2,1)S(1)}, u32[]{:S(2)}, u32[]{:S(2)}) collective-permute-start(bf16[2,256,512]{2,1,0:T(8,128)(2,1)S(1)} %copy-done), channel_id=1, source_target_pairs={{0,2},{1,3},{2,0},{3,1},{4,6},{5,7},{6,4},{7,5},{8,10},{9,11},{10,... | collective-permute-start | bytes 1572872 | tf_op jit(solution)/shard_map/ppermute | solution.py:198
  85.5 1.1 collective-permute-start.2
  86.6 0.0 collective-permute-done.4
  86.7 0.8 copy_bitcast_fusion
  87.5 22.6 %collective-permute-done.refs_1_ = bf16[2,256,512]{2,1,0:T(8,128)(2,1)S(1)} collective-permute-done((bf16[2,256,512]{2,1,0:T(8,128)(2,1)S(1)}, bf16[2,256,512]{2,1,0:T(8,128)(2,1)S(1)}, u32[]{:S(2)}, u32[]{:S(2)}) %collective-permute-start) | collective-permute-done | bytes 524320 | tf_op jit(solution)/shard_map/ppermute | solution.py:198
  110.1 0.0 copy-start.1
  110.1 0.0 collective-permute-done.1.refs_2_
  110.1 0.0 copy-start.2
  110.1 0.3 collective-permute-done.2.refs_3_
  110.4 0.0 copy-start.3
  110.4 0.5 copy-done.1
  110.9 0.2 copy-done.2
  111.1 0.2 copy-done.3
  111.2 14.9 %all-gather.3.cloned.1.call-done = bf16[128,128,512]{2,1,0:T(8,128)(2,1)} async-done(((bf16[2,128,512]{2,1,0:T(8,128)(2,1)}), bf16[128,128,512]{2,1,0:T(8,128)(2,1)}) %all-gather.3.cloned.1.call-update) | async-done | bytes 16777232 | tf_op jit(solution)/shard_map/all_gather | solution.py:192
  126.1 10.2 %shard_map.113 = bf16[2,256,2048]{2,1,0:T(8,128)(2,1)} custom-call(s32[1]{0:T(128)} %bitcast.y_ref, bf16[2,256,512]{2,1,0:T(8,128)(2,1)} %get-tuple-element.16.f0, bf16[2,256,512]{2,1,0:T(8,128)(2,1)} %get-tuple-element.17.f1, bf16[2,256,512]{2,1,0:T(8,128)(2,1)} %get-tuple-element.18.f2, bf16[2,256,512]{2,1,0:T(8,128)(2,1)} %get-tuple-element.19.f3, ...), custom_call_target="tpu_custom_call" | custom-call | flops 2000000000 | bytes 16000000 | tf_op jit(solution)/shard_map/pallas_call | solution.py:119
  (4 shorter events, 0.1 us)
Async XLA Ops:
  7.2 119.0 %all-gather.3.cloned.1.call-start = ((), (), s32[]{:S(2)}) async-start(), calls=%async_computation.2 | async-start | bytes 17039360 | tf_op jit(solution)/shard_map/all_gather | solution.py:192
  8.2 9.4 %collective-permute-start.5 = (bf16[2,128,512]{2,1,0:T(8,128)(2,1)S(1)}, bf16[2,128,512]{2,1,0:T(8,128)(2,1)S(1)}, u32[]{:S(2)}, u32[]{:S(2)}) collective-permute-start(bf16[2,128,512]{2,1,0:T(8,128)(2,1)S(1)} %pad_maximum_fusion), channel_id=1, source_target_pairs={{0,0},{1,64},{2,128},{3,192},{4,132},{5,196},{6,4},{7,68},{64,1},{... | collective-permute-start | bytes 786440 | tf_op jit(solution)/shard_map/ppermute | solution.py:164
  17.6 0.7 copy-start.4
  37.1 46.8 %copy-start = (bf16[2,256,512]{2,1,0:T(8,128)(2,1)S(1)}, bf16[2,256,512]{2,1,0:T(8,128)(2,1)}, u32[]{:S(2)}) copy-start(bf16[2,256,512]{2,1,0:T(8,128)(2,1)} %get-tuple-element.14.refs_0_) | copy-start | bytes 1572868
  38.2 1.6 %collective-permute-start.3 = (f32[2,2,128,128]{3,2,1,0:T(8,128)S(1)}, f32[2,2,128,128]{3,2,1,0:T(8,128)S(1)}, u32[]{:S(2)}, u32[]{:S(2)}) collective-permute-start(f32[2,2,128,128]{3,2,1,0:T(8,128)S(1)} %select_bitcast_fusion), channel_id=1, source_target_pairs={{0,4},{4,0},{1,5},{5,1},{2,6},{6,2},{3,7},{7,3},{8,12},{12,8},{9,1... | collective-permute-start | bytes 786440 | tf_op jit(solution)/shard_map/ppermute | solution.py:154
  81.2 5.5 %collective-permute-start.4 = (bf16[512,128]{1,0:T(8,128)(2,1)S(1)}, bf16[512,128]{1,0:T(8,128)(2,1)S(1)}, u32[]{:S(2)}, u32[]{:S(2)}) collective-permute-start(bf16[512,128]{1,0:T(8,128)(2,1)S(1)} %bitcast.36), channel_id=1, source_target_pairs={{0,4},{4,0},{1,5},{5,1},{2,6},{6,2},{3,7},{7,3},{8,12},{12,8},{9,1... | collective-permute-start | bytes 393224 | tf_op jit(solution)/shard_map/ppermute | solution.py:154
  83.9 26.1 %collective-permute-start = (bf16[2,256,512]{2,1,0:T(8,128)(2,1)S(1)}, bf16[2,256,512]{2,1,0:T(8,128)(2,1)S(1)}, u32[]{:S(2)}, u32[]{:S(2)}) collective-permute-start(bf16[2,256,512]{2,1,0:T(8,128)(2,1)S(1)} %copy-done), channel_id=1, source_target_pairs={{0,1},{1,2},{2,3},{3,0},{4,5},{5,6},{6,7},{7,4},{8,9},{9,10},{10,1... | collective-permute-start | bytes 1572872 | tf_op jit(solution)/shard_map/ppermute | solution.py:198
  83.9 26.1 %collective-permute-start.1 = (bf16[2,256,512]{2,1,0:T(8,128)(2,1)S(1)}, bf16[2,256,512]{2,1,0:T(8,128)(2,1)S(1)}, u32[]{:S(2)}, u32[]{:S(2)}) collective-permute-start(bf16[2,256,512]{2,1,0:T(8,128)(2,1)S(1)} %copy-done), channel_id=1, source_target_pairs={{0,2},{1,3},{2,0},{3,1},{4,6},{5,7},{6,4},{7,5},{8,10},{9,11},{10,... | collective-permute-start | bytes 1572872 | tf_op jit(solution)/shard_map/ppermute | solution.py:198
  85.5 24.8 %collective-permute-start.2 = (bf16[2,256,512]{2,1,0:T(8,128)(2,1)S(1)}, bf16[2,256,512]{2,1,0:T(8,128)(2,1)S(1)}, u32[]{:S(2)}, u32[]{:S(2)}) collective-permute-start(bf16[2,256,512]{2,1,0:T(8,128)(2,1)S(1)} %copy-done), channel_id=1, source_target_pairs={{0,3},{1,0},{2,1},{3,2},{4,7},{5,4},{6,5},{7,6},{8,11},{9,8},{10,9... | collective-permute-start | bytes 1572872 | tf_op jit(solution)/shard_map/ppermute | solution.py:198
  110.1 0.8 copy-start.1
  110.1 1.0 copy-start.2
  110.4 0.9 copy-start.3
Sparse Core Ops, SparseCore 0:
  18.5 107.6 all-gather.2

commit v5 on v4

--- a/solution.py
+++ b/solution.py
@@ -107,7 +107,7 @@
 def project(flats, weights, y):
     layers, tokens, depth = flats[0].shape
     rows = weights.shape[4]
-    step = 4
+    step = 8
     flat_spec = pl.BlockSpec((1, tokens, depth), lambda l, n, y_ref: (l, 0, 0))
 
     def weight_spec(s, core):

time: 143 us -> 143 us (level)
  no operation moved by 1% of the time
where the time goes in v5:
time: 143 us
  waiting for transfers between devices  43.2 us (30%)
  blocking collectives  40.2 us (28%)
  Pallas kernels  28.6 us (20%)
  between operations  14.1 us (10%)
  starting transfers between devices  11.1 us (8%)
  other arithmetic  4.1 us (3%)
  local copies, waits for them, and re-layouts  1.6 us (1%)
    all_to_all x2, blocking collectives, exchange(): return lax.all_to_all(a, ('x', 'z'), 0, 0, tiled=True)  40.2 us
    ppermute x3, waiting for transfers between devices, shards(): flats = [flat] + [lax.ppermute(flat, 'y', ring(4, q)) for q in (1, 2, 3)]  22.9 us
    pallas_call x1, Pallas kernels, attend_back(): pl.pallas_call(attend_kernel, grid=(layers, heads), in_specs=[wide, own,...  18.8 us
    all_gather x1, waiting for transfers between devices, shards(): weights = lax.all_gather(turned, ('x', 'z', 'core'), axis=0)  14.9 us
    pallas_call x1, Pallas kernels, project(): pl.pallas_call(project_kernel, grid_spec=pltpu.PrefetchScalarGridSpec(num...  9.86 us
    ppermute x1, starting transfers between devices, turn(): return lax.ppermute(a, ('x', 'core', 'y'), pairs)  5.48 us
    ppermute x1, waiting for transfers between devices, turn(): return lax.ppermute(a, ('x', 'core', 'y'), pairs)  3.92 us
    ppermute x2, starting transfers between devices, swap_cores(): return lax.ppermute(a, 'core', [(0, 1), (1, 0)])  2.86 us
  transfers between devices with their start and end apart: 7, of which 5 were waited for; matrix products, arithmetic and copies ran while one was open for 2% of the time, Pallas kernels for 13%

profile of v5, /device:TPU:1, one launch (start us, length us, event | category | flops | bytes accessed | tf_op | source)
XLA Modules:
  0.0 142.8 jit_solution(11903622453657796499)
XLA Ops:
  7.2 0.0 all-gather.3.cloned.1.call-start
  7.2 1.0 pad_maximum_fusion
  8.2 5.5 %collective-permute-start.5 = (bf16[2,128,512]{2,1,0:T(8,128)(2,1)S(1)}, bf16[2,128,512]{2,1,0:T(8,128)(2,1)S(1)}, u32[]{:S(2)}, u32[]{:S(2)}) collective-permute-start(bf16[2,128,512]{2,1,0:T(8,128)(2,1)S(1)} %pad_maximum_fusion), channel_id=1, source_target_pairs={{0,0},{1,64},{2,128},{3,192},{4,132},{5,196},{6,4},{7,68},{64,1},{... | collective-permute-start | bytes 786440 | tf_op jit(solution)/shard_map/ppermute | solution.py:164
  13.7 3.9 %collective-permute-done.5 = bf16[2,128,512]{2,1,0:T(8,128)(2,1)S(1)} collective-permute-done((bf16[2,128,512]{2,1,0:T(8,128)(2,1)S(1)}, bf16[2,128,512]{2,1,0:T(8,128)(2,1)S(1)}, u32[]{:S(2)}, u32[]{:S(2)}) %collective-permute-start.5) | collective-permute-done | bytes 262176 | tf_op jit(solution)/shard_map/ppermute | solution.py:164
  17.6 0.0 copy-start.4
  17.6 0.7 copy-done.4
  18.3 0.0 all-gather.3.cloned.1.call-update
  18.3 18.8 %shard_map.111 = (bf16[2,256,2048]{2,1,0:T(8,128)(2,1)}, bf16[2,256,512]{2,1,0:T(8,128)(2,1)}, f32[2,2,2,128,128]{4,3,2,1,0:T(8,128)}) custom-call(bf16[2,256,2048]{2,1,0:T(8,128)(2,1)} %q_ref.1, bf16[2,256,256]{2,1,0:T(8,128)(2,1)} %k_ref.1, bf16[2,256,256]{2,1,0:T(8,128)(2,1)} %v_ref.1, bf16[2,128,256]{2,1,0:T(8,128)(2,1)} %pk_ref.1, ...), custom_call_target="tpu_custom_call" | custom-call | flops 2000000000 | bytes 16000000 | tf_op jit(solution)/shard_map/pallas_call | solution.py:81
  37.1 0.0 copy-start
  37.1 1.1 select_bitcast_fusion
  38.2 0.1 collective-permute-start.3
  38.3 1.5 %collective-permute-done.3 = f32[2,2,128,128]{3,2,1,0:T(8,128)S(1)} collective-permute-done((f32[2,2,128,128]{3,2,1,0:T(8,128)S(1)}, f32[2,2,128,128]{3,2,1,0:T(8,128)S(1)}, u32[]{:S(2)}, u32[]{:S(2)}) %collective-permute-start.3) | collective-permute-done | bytes 262176 | tf_op jit(solution)/shard_map/ppermute | solution.py:154
  39.9 1.1 fusion
  40.9 26.2 %all_to_all.18 = bf16[32,16,128]{2,1,0:T(8,128)(2,1)S(1)} all-to-all(bf16[32,16,128]{2,1,0:T(8,128)(2,1)S(1)} %bitcast.37), channel_id=1, replica_groups=mesh['x'=4,'z'=8,'core'=2,'y'=4] {'x','z'}, dimensions={0} | all-to-all | bytes 262144 | tf_op jit(solution)/shard_map/all_to_all | solution.py:168
  67.2 14.0 %all_to_all.19 = bf16[32,16,128]{2,1,0:T(8,128)(2,1)S(1)} all-to-all(bf16[32,16,128]{2,1,0:T(8,128)(2,1)S(1)} %broadcast_in_dim.2), channel_id=1, replica_groups=mesh['x'=4,'z'=8,'core'=2,'y'=4] {'x','z'}, dimensions={0} | all-to-all | bytes 262144 | tf_op jit(solution)/shard_map/all_to_all | solution.py:168
  81.2 2.8 %collective-permute-start.4 = (bf16[512,128]{1,0:T(8,128)(2,1)S(1)}, bf16[512,128]{1,0:T(8,128)(2,1)S(1)}, u32[]{:S(2)}, u32[]{:S(2)}) collective-permute-start(bf16[512,128]{1,0:T(8,128)(2,1)S(1)} %bitcast.36), channel_id=1, source_target_pairs={{0,4},{4,0},{1,5},{5,1},{2,6},{6,2},{3,7},{7,3},{8,12},{12,8},{9,1... | collective-permute-start | bytes 393224 | tf_op jit(solution)/shard_map/ppermute | solution.py:154
  83.9 0.0 copy-done
  83.9 0.0 collective-permute-start
  83.9 1.6 %collective-permute-start.1 = (bf16[2,256,512]{2,1,0:T(8,128)(2,1)S(1)}, bf16[2,256,512]{2,1,0:T(8,128)(2,1)S(1)}, u32[]{:S(2)}, u32[]{:S(2)}) collective-permute-start(bf16[2,256,512]{2,1,0:T(8,128)(2,1)S(1)} %copy-done), channel_id=1, source_target_pairs={{0,2},{1,3},{2,0},{3,1},{4,6},{5,7},{6,4},{7,5},{8,10},{9,11},{10,... | collective-permute-start | bytes 1572872 | tf_op jit(solution)/shard_map/ppermute | solution.py:198
  85.5 1.1 collective-permute-start.2
  86.6 0.0 collective-permute-done.4
  86.7 0.8 copy_bitcast_fusion
  87.5 22.6 %collective-permute-done.refs_1_ = bf16[2,256,512]{2,1,0:T(8,128)(2,1)S(1)} collective-permute-done((bf16[2,256,512]{2,1,0:T(8,128)(2,1)S(1)}, bf16[2,256,512]{2,1,0:T(8,128)(2,1)S(1)}, u32[]{:S(2)}, u32[]{:S(2)}) %collective-permute-start) | collective-permute-done | bytes 524320 | tf_op jit(solution)/shard_map/ppermute | solution.py:198
  110.1 0.0 copy-start.1
  110.1 0.0 collective-permute-done.1.refs_2_
  110.1 0.0 copy-start.2
  110.1 0.3 collective-permute-done.2.refs_3_
  110.4 0.0 copy-start.3
  110.4 0.5 copy-done.1
  110.9 0.2 copy-done.2
  111.1 0.2 copy-done.3
  111.2 14.9 %all-gather.3.cloned.1.call-done = bf16[128,128,512]{2,1,0:T(8,128)(2,1)} async-done(((bf16[2,128,512]{2,1,0:T(8,128)(2,1)}), bf16[128,128,512]{2,1,0:T(8,128)(2,1)}) %all-gather.3.cloned.1.call-update) | async-done | bytes 16777232 | tf_op jit(solution)/shard_map/all_gather | solution.py:192
  126.1 9.9 %shard_map.113 = bf16[2,256,2048]{2,1,0:T(8,128)(2,1)} custom-call(s32[1]{0:T(128)} %bitcast.y_ref, bf16[2,256,512]{2,1,0:T(8,128)(2,1)} %get-tuple-element.16.f0, bf16[2,256,512]{2,1,0:T(8,128)(2,1)} %get-tuple-element.17.f1, bf16[2,256,512]{2,1,0:T(8,128)(2,1)} %get-tuple-element.18.f2, bf16[2,256,512]{2,1,0:T(8,128)(2,1)} %get-tuple-element.19.f3, ...), custom_call_target="tpu_custom_call" | custom-call | flops 2000000000 | bytes 16000000 | tf_op jit(solution)/shard_map/pallas_call | solution.py:119
  (4 shorter events, 0.1 us)
Async XLA Ops:
  7.2 119.0 %all-gather.3.cloned.1.call-start = ((), (), s32[]{:S(2)}) async-start(), calls=%async_computation.2 | async-start | bytes 17039360 | tf_op jit(solution)/shard_map/all_gather | solution.py:192
  8.2 9.4 %collective-permute-start.5 = (bf16[2,128,512]{2,1,0:T(8,128)(2,1)S(1)}, bf16[2,128,512]{2,1,0:T(8,128)(2,1)S(1)}, u32[]{:S(2)}, u32[]{:S(2)}) collective-permute-start(bf16[2,128,512]{2,1,0:T(8,128)(2,1)S(1)} %pad_maximum_fusion), channel_id=1, source_target_pairs={{0,0},{1,64},{2,128},{3,192},{4,132},{5,196},{6,4},{7,68},{64,1},{... | collective-permute-start | bytes 786440 | tf_op jit(solution)/shard_map/ppermute | solution.py:164
  17.6 0.7 copy-start.4
  37.1 46.8 %copy-start = (bf16[2,256,512]{2,1,0:T(8,128)(2,1)S(1)}, bf16[2,256,512]{2,1,0:T(8,128)(2,1)}, u32[]{:S(2)}) copy-start(bf16[2,256,512]{2,1,0:T(8,128)(2,1)} %get-tuple-element.14.refs_0_) | copy-start | bytes 1572868
  38.2 1.6 %collective-permute-start.3 = (f32[2,2,128,128]{3,2,1,0:T(8,128)S(1)}, f32[2,2,128,128]{3,2,1,0:T(8,128)S(1)}, u32[]{:S(2)}, u32[]{:S(2)}) collective-permute-start(f32[2,2,128,128]{3,2,1,0:T(8,128)S(1)} %select_bitcast_fusion), channel_id=1, source_target_pairs={{0,4},{4,0},{1,5},{5,1},{2,6},{6,2},{3,7},{7,3},{8,12},{12,8},{9,1... | collective-permute-start | bytes 786440 | tf_op jit(solution)/shard_map/ppermute | solution.py:154
  81.2 5.5 %collective-permute-start.4 = (bf16[512,128]{1,0:T(8,128)(2,1)S(1)}, bf16[512,128]{1,0:T(8,128)(2,1)S(1)}, u32[]{:S(2)}, u32[]{:S(2)}) collective-permute-start(bf16[512,128]{1,0:T(8,128)(2,1)S(1)} %bitcast.36), channel_id=1, source_target_pairs={{0,4},{4,0},{1,5},{5,1},{2,6},{6,2},{3,7},{7,3},{8,12},{12,8},{9,1... | collective-permute-start | bytes 393224 | tf_op jit(solution)/shard_map/ppermute | solution.py:154
  83.9 26.1 %collective-permute-start = (bf16[2,256,512]{2,1,0:T(8,128)(2,1)S(1)}, bf16[2,256,512]{2,1,0:T(8,128)(2,1)S(1)}, u32[]{:S(2)}, u32[]{:S(2)}) collective-permute-start(bf16[2,256,512]{2,1,0:T(8,128)(2,1)S(1)} %copy-done), channel_id=1, source_target_pairs={{0,1},{1,2},{2,3},{3,0},{4,5},{5,6},{6,7},{7,4},{8,9},{9,10},{10,1... | collective-permute-start | bytes 1572872 | tf_op jit(solution)/shard_map/ppermute | solution.py:198
  83.9 26.1 %collective-permute-start.1 = (bf16[2,256,512]{2,1,0:T(8,128)(2,1)S(1)}, bf16[2,256,512]{2,1,0:T(8,128)(2,1)S(1)}, u32[]{:S(2)}, u32[]{:S(2)}) collective-permute-start(bf16[2,256,512]{2,1,0:T(8,128)(2,1)S(1)} %copy-done), channel_id=1, source_target_pairs={{0,2},{1,3},{2,0},{3,1},{4,6},{5,7},{6,4},{7,5},{8,10},{9,11},{10,... | collective-permute-start | bytes 1572872 | tf_op jit(solution)/shard_map/ppermute | solution.py:198
  85.5 24.8 %collective-permute-start.2 = (bf16[2,256,512]{2,1,0:T(8,128)(2,1)S(1)}, bf16[2,256,512]{2,1,0:T(8,128)(2,1)S(1)}, u32[]{:S(2)}, u32[]{:S(2)}) collective-permute-start(bf16[2,256,512]{2,1,0:T(8,128)(2,1)S(1)} %copy-done), channel_id=1, source_target_pairs={{0,3},{1,0},{2,1},{3,2},{4,7},{5,4},{6,5},{7,6},{8,11},{9,8},{10,9... | collective-permute-start | bytes 1572872 | tf_op jit(solution)/shard_map/ppermute | solution.py:198
  110.1 0.8 copy-start.1
  110.1 1.0 copy-start.2
  110.4 0.9 copy-start.3
Sparse Core Ops, SparseCore 0:
  18.5 107.6 all-gather.2
